TPU v7x, 32 devices: a whole 2x2x4 slice. The times are simulated.
32 devices in a mesh: group: 2 (over y), dm: 4 (over z), tm: 2 (over x), beam: 2 (over core).
Axes of the slice: x: 2, y: 2, z: 4, core: 2. Of those that a mesh axis runs over, the one named last changes fastest.
Arguments:
- raw: bfloat16 [16, 4194304], P(('group', 'dm', 'beam'), 'tm'), parts along dimension 0
- proto: float32 [4, 16384], replicated, may hold values from -4 to 4
- delays: int32 [8, 4, 64], replicated, may hold values from 0 to 3, as said below
- widths: int32 [8], replicated, may hold values from 1 to 8, as said below
- owners: int32 [8, 1], replicated, may hold values from 0 to 3; in each aligned block of 8 rows (0 to 7, 8 to 15, ...) at most 4 rows name the same one
Outputs:
- detect: bfloat16 [16, 8, 2, 4, 8, 256], P('dm', 'group', 'beam', None, None, 'tm'), parts along dimension 1
There are 2 independent parts, one for each index of `group`. A program takes and returns all parts, laid end to end along the dimension named above; an argument that names none is the same for every part. Nothing has to cross between parts.
Inputs may be any that keep to these rules, and one draw needn't show every extreme that they name: `delays`: 3 occurs in every draw. `widths`: 8 occurs in every draw. `owners`: each owner holds at most 4 DM blocks, and some owner holds exactly 4.
All inputs are finite; a program needn't handle non-finite values.
Results may differ from a plain program's by a relative error of at most 0.014.
Values may be sent and summed in bfloat16 or wider, within the bound.
A program may use at most 128 MiB of HBM per device.

v0:
```python
import functools
import math

import jax
import jax.numpy as jnp
import numpy as np
from jax import lax
from jax.experimental import pallas as pl
from jax.experimental.pallas import tpu as pltpu
from jax.sharding import PartitionSpec as P

SIDE = 128
NBLK = 64
FD = 4
TT = 8
MAXT = 3
WMAX = 8
SPB = 32
HALF = SIDE // 2
FR = 80
MESH = pl.DeviceIdType.MESH
F32 = jnp.float32
BF16 = jnp.bfloat16


def tables(channels):
    i = np.arange(SIDE)
    ang = (i[:, None] * i[None, :] % SIDE) * (2.0 * math.pi / SIDE)
    c, s = np.cos(ang), np.sin(ang)
    w1 = np.concatenate([c[:FR], s[:FR]], 0)
    w2 = np.block([[c, -s], [-s, -c]])
    tw = (i[:, None] * i[None, :] % channels) * (2.0 * math.pi / channels)
    twiddle = np.stack([np.cos(tw[:FR]), np.sin(tw[:FR])]).astype(np.float32)
    return jnp.asarray(w1, BF16), jnp.asarray(w2, BF16), jnp.asarray(twiddle)


def fine_rows(groups, width):
    g = np.arange(groups)[:, None]
    i = np.arange(width)[None, :]
    fine = g * FD * (width - 1 - i) // (groups * (width - 1))
    hot = np.stack([fine == step for step in range(FD)])
    hot = hot.reshape(FD, groups, width // SIDE, SIDE).transpose(2, 0, 1, 3)
    out = np.zeros((2, 2, FD, groups, FR))
    out[0, ..., : HALF + 1] = hot[..., : HALF + 1]
    out[1, ..., 1:HALF] = hot[..., : HALF : -1]
    return jnp.asarray(out.reshape(-1, FR), BF16)


def search_kernel(
    sizes, x_ref, raw_ref, proto_ref, w1_ref, w2_ref, tw_ref, m_ref, delays_ref, widths_ref, owners_ref, out_ref,
    window, early, history, filt, p_ref, band_ref, bands, inv, direct, mirror, tot, tail, send, got,
    hist_send, hist_recv, band_send, band_recv, tail_send, tail_recv, own_send, own_recv,
):
    spectra, spec, groups, slabs, owner_count, axes = sizes
    step = pl.program_id(0)
    scale = 1.0 / (4 * SIDE * SIDE)
    frame_size = SIDE * SIDE
    tm = lax.axis_index("tm")

    def peer(axis, shift):
        place = {name: lax.axis_index(name) for name in axes}
        place[axis] = lax.rem(place[axis] + shift, lax.axis_size(axis))
        return tuple(place[name] for name in axes)

    def history_copy():
        size = history.shape[1]
        return pltpu.make_async_remote_copy(
            src_ref=raw_ref.at[:, pl.ds(spec * frame_size - size, size)],
            dst_ref=history,
            send_sem=hist_send,
            recv_sem=hist_recv,
            device_id=peer("tm", 1),
            device_id_type=MESH,
        )

    def unfold(ref, index):
        line = ref[:, index * frame_size : (index + 1) * frame_size]
        return line.astype(F32).reshape(SIDE, SIDE)

    def pair(win, s, start):
        ys = []
        for k in (s, s + 1):
            acc = win[k * SIDE : (k + 1) * SIDE] * filt[0]
            for tap in range(1, 4):
                acc = acc + win[(k + tap) * SIDE : (k + tap + 1) * SIDE] * filt[tap]
            ys.append(acc.astype(BF16))
        a = jnp.dot(w1_ref[...], jnp.concatenate(ys, 1), preferred_element_type=F32)
        ts = []
        for m in range(2):
            re = a[:FR, m * SIDE : (m + 1) * SIDE]
            im = a[FR:, m * SIDE : (m + 1) * SIDE]
            t_re = re * tw_ref[0] - im * tw_ref[1]
            t_ni = im * tw_ref[0] + re * tw_ref[1]
            ts.append(jnp.concatenate([t_re.astype(BF16), t_ni.astype(BF16)], 1))
        c = jnp.dot(jnp.concatenate(ts, 0), w2_ref[...], preferred_element_type=F32)
        re, im = c[:, :SIDE], c[:, SIDE:]
        power = (re * re + im * im) * scale
        p_ref[pl.ds(start, 2 * FR)] = power
        band_ref[...] += power[:FR] + power[FR:]

    @pl.when(step == 0)
    def _():
        barrier = pltpu.get_barrier_semaphore()
        for off in range(1, slabs):
            pl.semaphore_signal(barrier, inc=1, device_id=peer("tm", off), device_id_type=MESH)
        for off in range(1, owner_count):
            pl.semaphore_signal(barrier, inc=1, device_id=peer("dm", off), device_id_type=MESH)
        pl.semaphore_wait(barrier, slabs + owner_count - 2)
        if slabs > 1:
            history_copy().start()
        for tap in range(4):
            filt[tap] = unfold(proto_ref.at[tap : tap + 1], 0)
        band_ref[...] = jnp.zeros_like(band_ref)
        direct[...] = jnp.zeros_like(direct)
        mirror[...] = jnp.zeros_like(mirror)
        for k in range(4):
            early[(k + 3) * SIDE : (k + 4) * SIDE] = unfold(x_ref, k)

    @pl.when(step > 0)
    def _():
        for k in range(4):
            window[(k + 3) * SIDE : (k + 4) * SIDE] = unfold(x_ref, k)
        for s in (0, 2):
            pair(window, s, pl.multiple_of((step * SPB + s) * FR, FR))

    @pl.when(step == 0)
    def _():
        window[4 * SIDE : 7 * SIDE] = early[4 * SIDE : 7 * SIDE]

    for k in range(4, SPB):
        window[(k + 3) * SIDE : (k + 4) * SIDE] = unfold(x_ref, k)
    for s in range(4, SPB, 2):
        pair(window, s, pl.multiple_of((step * SPB + s) * FR, FR))
    window[: 3 * SIDE] = window[SPB * SIDE :]

    @pl.when(step == spec // SPB - 1)
    def _():
        if slabs > 1:
            history_copy().wait()
            for k in range(3):
                early[k * SIDE : (k + 1) * SIDE] = jnp.where(tm > 0, unfold(history, k), 0.0)
        else:
            early[: 3 * SIDE] = jnp.zeros((3 * SIDE, SIDE), F32)
        for s in (0, 2):
            pair(early, s, s * FR)
        finish(
            sizes, peer, m_ref, delays_ref, widths_ref, owners_ref, out_ref,
            p_ref, band_ref, bands, inv, direct, mirror, tot, tail, send, got,
            band_send, band_recv, tail_send, tail_recv, own_send, own_recv,
        )


def finish(
    sizes, peer, m_ref, delays_ref, widths_ref, owners_ref, out_ref,
    p_ref, band_ref, bands, inv, direct, mirror, tot, tail, send, got,
    band_send, band_recv, tail_send, tail_recv, own_send, own_recv,
):
    spectra, spec, groups, slabs, owner_count, axes = sizes
    halo = MAXT * TT + WMAX - 1
    slots = out_ref.shape[0]
    trials = out_ref.shape[2] // widths_ref.shape[1]
    quad = trials * groups
    tm, dm = lax.axis_index("tm"), lax.axis_index("dm")

    copies = []
    for off in range(1, slabs):
        copy = pltpu.make_async_remote_copy(
            src_ref=band_ref,
            dst_ref=bands.at[off - 1],
            send_sem=band_send.at[off - 1],
            recv_sem=band_recv.at[off - 1],
            device_id=peer("tm", off),
            device_id_type=MESH,
        )
        copy.start()
        copies.append(copy)
    iota = lambda shape, dim: lax.broadcasted_iota(jnp.int32, shape, dim)
    spread = (iota((NBLK, SIDE), 1) == 2 * iota((NBLK, SIDE), 0)).astype(BF16)
    late = jnp.dot(delays_ref[...].astype(F32).astype(BF16), spread, preferred_element_type=F32)
    on = iota((quad, SIDE), 1) % 2 == 0
    mask = jnp.concatenate(
        [jnp.where(on & (late == float(v)), 1.0, 0.0) for v in range(MAXT + 1)], 0
    ).astype(BF16)
    def column(ref):
        n = ref.shape[1]
        same = iota((n, n), 0) == iota((n, n), 1)
        return jnp.sum(jnp.where(same, jnp.broadcast_to(ref[...], (n, n)), 0), 1, keepdims=True)

    wide = max(SIDE, quad)
    lane = iota((groups, wide), 1)
    row = iota((groups, wide), 0)
    owner = jnp.broadcast_to(column(owners_ref), (groups, wide))
    mine = jnp.sum(jnp.where(lane // trials == row, owner, 0), 0, keepdims=True)
    rank = jnp.sum(jnp.where((owner == mine) & (row < lane // trials), 1, 0), 0, keepdims=True)
    place = (mine * slots + rank) * trials + lane[:1] % trials
    place = jnp.where(lane[:1] < quad, place, -1)
    rows_out = owner_count * slots * trials
    pack = jnp.where(iota((rows_out, wide), 0) == place, 1.0, 0.0)
    reach = jnp.broadcast_to(column(widths_ref), (widths_ref.shape[1], SIDE))
    root = 1.0 / jnp.sqrt(reach.astype(F32))
    weights = [jnp.where(reach > lag, root, 0.0) for lag in range(WMAX)]

    band = band_ref[...]
    for off in range(1, slabs):
        copies[off - 1].wait()
        band = band + bands[off - 1]
    held = lax.broadcasted_iota(jnp.int32, (FR, SIDE), 0) <= HALF
    inv[...] = jnp.where(held, 1.0 / (band * (1.0 / spectra) + 1e-06), 0.0)

    even = lax.broadcasted_iota(jnp.int32, (FD * groups, SIDE), 1) % 2 == 0

    def block(step, carry):
        for s in range(0, SPB, 2):
            flats = []
            for k in (s, s + 1):
                start = pl.multiple_of((step * SPB + k) * FR, FR)
                ratio = p_ref[pl.ds(start, FR)] * inv[...]
                line = 2.0 * jnp.sum(ratio, 0, keepdims=True) - ratio[:1] - ratio[HALF : HALF + 1]
                mean = jnp.sum(line, 1, keepdims=True) * (1.0 / (SIDE * SIDE))
                flats.append((ratio - mean).astype(BF16))
            r = jnp.dot(m_ref[...], jnp.concatenate(flats, 1), preferred_element_type=F32)
            size = FD * groups
            for m in range(2):
                part = r[:, m * SIDE : (m + 1) * SIDE]
                one = jnp.where(even, part[:size], part[size : 2 * size])
                two = jnp.where(even, part[3 * size :], part[2 * size : 3 * size])
                for d in range(FD):
                    direct[step * SPB + s + m + d] += one[d * groups : (d + 1) * groups]
                    mirror[step * SPB + s + m + d] += two[d * groups : (d + 1) * groups]
        return carry

    def combine(first, stop):
        one = direct[first:stop].reshape(-1, SIDE)
        two = mirror[first:stop].reshape(-1, SIDE)
        high = two.astype(BF16)
        low = (two - high.astype(F32)).astype(BF16)
        both = jnp.concatenate([high, low], 1)
        turned = jnp.dot(both, turn, preferred_element_type=F32)
        total = one + pltpu.roll(one, SIDE - 1, 1) + turned
        tot[first:stop] = total.reshape(stop - first, groups, SIDE)

    source = iota((2 * SIDE, SIDE), 0) % SIDE
    goal = iota((2 * SIDE, SIDE), 1)
    turn = jnp.where((goal % 2 == 0) & (source // 2 == HALF - 1 - goal // 2), 1.0, 0.0).astype(BF16)
    blocks = spec // SPB
    last = -(-(halo + FD - 1) // SPB)
    lax.fori_loop(blocks - last, blocks, block, 0)
    combine(spec - halo, spec + FD - 1)
    if slabs > 1:
        tail_copy = pltpu.make_async_remote_copy(
            src_ref=tot.at[pl.ds(spec - halo, halo + FD - 1)],
            dst_ref=tail,
            send_sem=tail_send,
            recv_sem=tail_recv,
            device_id=peer("tm", 1),
            device_id_type=MESH,
        )
        tail_copy.start()
        lax.fori_loop(0, blocks - last, block, 0)
        combine(0, spec - halo)
        tail_copy.wait()
        before = jnp.where(tm > 0, tail[...], 0.0)
    else:
        lax.fori_loop(0, blocks - last, block, 0)
        combine(0, spec - halo)
        before = jnp.zeros(tail.shape, F32)

    rows = spec + halo + 1
    ext = jnp.concatenate(
        [
            jnp.zeros((1, groups, SIDE), F32),
            before[:halo],
            tot[: FD - 1] + before[halo:],
            tot[FD - 1 : spec],
        ],
        0,
    ).reshape(rows * groups, SIDE)
    width = SIDE * SIDE // NBLK
    sub = (ext * (1.0 / math.sqrt(width))).astype(BF16)
    prod = lax.dot_general(
        sub, mask, (((1,), (1,)), ((), ())), preferred_element_type=F32
    )
    lanes = prod.shape[1]
    prod = prod.reshape(rows, groups, lanes)
    lane = lax.broadcasted_iota(jnp.int32, (groups, lanes), 1)
    row = lax.broadcasted_iota(jnp.int32, (groups, lanes), 0)
    own = (lane // trials) % groups == row
    each = jnp.sum(jnp.where(own[None], prod, 0.0), 1)
    count = spec + TT
    dd = 0.0
    for value in range(MAXT + 1):
        start = (MAXT - value) * TT
        dd = dd + each[start : start + count, value * quad : (value + 1) * quad]
    dd = dd * (1.0 / math.sqrt(NBLK))
    if quad < wide:
        dd = jnp.concatenate([dd, jnp.zeros((count, wide - quad), F32)], 1)
    dd = jnp.concatenate([dd, jnp.zeros((2 * SIDE - count, wide), F32)], 0)
    packed = jnp.dot(
        pack, dd.T, preferred_element_type=F32, precision=lax.Precision.HIGHEST
    )
    send[...] = packed.reshape(send.shape)

    copies = []
    for off in range(1, owner_count):
        copy = pltpu.make_async_remote_copy(
            src_ref=send.at[lax.rem(dm + off, owner_count)],
            dst_ref=got.at[dm],
            send_sem=own_send.at[off - 1],
            recv_sem=own_recv.at[off - 1],
            device_id=peer("dm", off),
            device_id_type=MESH,
        )
        copy.start()
        copies.append(copy)
    got[dm] = send[dm]
    for copy in copies:
        copy.wait()

    for d in range(owner_count):
        part = got[d]
        acc = 0.0
        for lag in range(WMAX):
            moved = pltpu.roll(part, 2 * SIDE - (TT - lag), 1)[:, :SIDE]
            acc = acc + moved[:, None, :] * weights[lag][None]
        for s in range(slots):
            part = acc[s * trials : (s + 1) * trials].reshape(-1, SIDE)
            out_ref[s, d] = part.astype(BF16)


def shards(axes, raw, proto, delays, widths, owners):
    taps, channels = proto.shape
    spec = raw.shape[1] // channels
    groups, trials, _ = delays.shape
    slabs, owner_count = lax.axis_size("tm"), lax.axis_size("dm")
    capacity = 2 * (groups // owner_count)
    halo = MAXT * TT + WMAX - 1
    w1, w2, tw = tables(channels)
    masks = fine_rows(groups, channels // NBLK)
    sizes = (spec * slabs, spec, groups, slabs, owner_count, axes)
    block = pltpu.VMEM((owner_count, capacity * trials, 2 * SIDE), F32)
    sems = lambda n: pltpu.SemaphoreType.DMA((max(n, 1),))
    full = lambda shape: pl.BlockSpec(shape, lambda i: (0,) * len(shape))
    small = [proto, w1, w2, tw, masks, delays.reshape(groups * trials, NBLK), widths[None], owners.T]
    out = (capacity, owner_count, trials * widths.shape[0], spec)
    box = pl.pallas_call(
        functools.partial(search_kernel, sizes),
        grid=(spec // SPB,),
        in_specs=[
            pl.BlockSpec((1, SPB * channels), lambda i: (0, i)),
            pl.BlockSpec(memory_space=pl.ANY),
            *[full(value.shape) for value in small],
        ],
        out_specs=full(out),
        out_shape=jax.ShapeDtypeStruct(out, BF16),
        scratch_shapes=[
            pltpu.VMEM(((SPB + 3) * SIDE, SIDE), F32),
            pltpu.VMEM((7 * SIDE, SIDE), F32),
            pltpu.VMEM((1, 3 * channels), BF16),
            pltpu.VMEM((taps, SIDE, SIDE), F32),
            pltpu.VMEM((spec * FR, SIDE), F32),
            pltpu.VMEM((FR, SIDE), F32),
            pltpu.VMEM((max(slabs - 1, 1), FR, SIDE), F32),
            pltpu.VMEM((FR, SIDE), F32),
            pltpu.VMEM((spec + FD - 1, groups, SIDE), F32),
            pltpu.VMEM((spec + FD - 1, groups, SIDE), F32),
            pltpu.VMEM((spec + FD - 1, groups, SIDE), F32),
            pltpu.VMEM((halo + FD - 1, groups, SIDE), F32),
            block,
            block,
            pltpu.SemaphoreType.DMA,
            pltpu.SemaphoreType.DMA,
            sems(slabs - 1),
            sems(slabs - 1),
            pltpu.SemaphoreType.DMA,
            pltpu.SemaphoreType.DMA,
            sems(owner_count - 1),
            sems(owner_count - 1),
        ],
        compiler_params=pltpu.CompilerParams(
            vmem_limit_bytes=56 << 20, collective_id=0, has_side_effects=True
        ),
        name="search",
    )(raw, raw, *small)
    return box.reshape(capacity, owner_count, 1, trials, widths.shape[0], spec)


def solution(mesh):
    return jax.shard_map(
        functools.partial(shards, mesh.axis_names),
        mesh=mesh,
        in_specs=(P(("group", "dm", "beam"), "tm"), P(), P(), P(), P()),
        out_specs=P("dm", "group", "beam", None, None, "tm"),
        check_vma=False,
    )
```

profile of v0, /device:TPU:0, one launch (start us, length us, event | category | flops | bytes accessed | tf_op | source)
XLA Modules:
  0.0 29.8 jit_solution(11133890146073481167)
XLA Ops:
  0.0 28.2 %search.1 = bf16[4,4,32,128]{3,2,1,0:T(8,128)(2,1)} custom-call(bf16[1,2097152]{1,0:T(2,128)(2,1)} %raw_ref.1, bf16[1,2097152]{1,0:T(2,128)(2,1)} %raw_ref.1, f32[4,16384]{1,0:T(4,128)} %proto_ref.1, bf16[160,128]{1,0:T(8,128)(2,1)} %constant.8.clone.w1_ref, bf16[256,256]{1,0:T(8,128)(2,1)} %constant.9.clone.w2_ref, f32[2,80,128]{2,1,0:T(8,128)} %constant.10.clone.tw_ref, ...), custom_call_target="tpu_custom_call" | custom-call | tf_op jit(solution)/shard_map/search/pallas_call | solution.py:345
  28.2 1.6 %copy.12 = bf16[4,4,1,4,8,128]{5,4,3,2,1,0:T(8,128)(2,1)} copy(bf16[4,4,1,4,8,128]{5,4,3,2,1,0:T(8,128)(2,1)} %bitcast.6) | data formatting | bytes 262144
where the time goes:
time: 29.9 us; the launch traced here: 29.8 us
  Pallas kernels  28.2 us (94%)
  local copies, waits for them, and re-layouts  1.57 us (5%)
    pallas_call x1, Pallas kernels, shards(): pl.pallas_call(functools.partial(search_kernel, sizes), grid=(spec // SPB...  28.2 us
    unnamed x1, local copies, waits for them, and re-layouts  1.57 us

commit v1 on v0

v1 whole, which is shorter than its diff:
```python
import functools
import math

import jax
import jax.numpy as jnp
import numpy as np
from jax import lax
from jax.experimental import pallas as pl
from jax.experimental.pallas import tpu as pltpu
from jax.sharding import PartitionSpec as P

SIDE = 128
NBLK = 64
FD = 4
TT = 8
MAXT = 3
WMAX = 8
SPB = 32
FIRST = 4
PIECE = 16
HALF = SIDE // 2
FR = 72
BACK = 128 - TT
MESH = pl.DeviceIdType.MESH
F32 = jnp.float32
BF16 = jnp.bfloat16


def tables(channels):
    i = np.arange(SIDE)
    ang = (i[:, None] * i[None, :] % SIDE) * (2.0 * math.pi / SIDE)
    c, s = np.cos(ang), np.sin(ang)
    w1 = np.concatenate([c[:FR], s[:FR]], 0)
    w2 = np.block([[c, -s], [-s, -c]])
    tw = (i[:, None] * i[None, :] % channels) * (2.0 * math.pi / channels)
    twiddle = np.stack([np.cos(tw[:FR]), np.sin(tw[:FR])]).astype(np.float32)
    return jnp.asarray(w1, BF16), jnp.asarray(w2, BF16), jnp.asarray(twiddle)


def fine_rows(groups, width):
    g = np.arange(groups)[:, None]
    i = np.arange(width)[None, :]
    fine = g * FD * (width - 1 - i) // (groups * (width - 1))
    hot = np.stack([fine == step for step in range(FD)])
    hot = hot.reshape(FD, groups, width // SIDE, SIDE).transpose(2, 0, 1, 3)
    out = np.zeros((2, 2, FD, groups, FR))
    out[0, ..., : HALF + 1] = hot[..., : HALF + 1]
    out[1, ..., 1:HALF] = hot[..., : HALF : -1]
    return jnp.asarray(out.reshape(-1, FR), BF16)


def iota(shape, dim):
    return lax.broadcasted_iota(jnp.int32, shape, dim)


def search_kernel(
    sizes, raw_ref, proto_ref, w1_any, w2_any, tw_any, m_any, delays_any, widths_any, owners_any, out_ref,
    xbuf, proto, w1_ref, w2_ref, tw_ref, m_ref, delays_ref, widths_ref, owners_ref,
    win, history, p_ref, band_ref, bands, inv, direct, mirror, send, sendb, got, gotb,
    raw_sem, proto_sem, const_sem,
    hist_send, hist_recv, band_send, band_recv, own_send, own_recv, next_send, next_recv,
):
    spectra, spec, groups, slabs, owner_count, axes = sizes
    frame = SIDE * SIDE
    slots = out_ref.shape[0]
    boxes = widths_ref.shape[1]
    trials = out_ref.shape[2] // boxes
    quad = trials * groups
    rows = slots * trials
    tm, dm = lax.axis_index("tm"), lax.axis_index("dm")

    def peer(slab, owner):
        place = {name: lax.axis_index(name) for name in axes}
        place["tm"] = lax.rem(tm + slab, slabs)
        place["dm"] = lax.rem(dm + owner, owner_count)
        return tuple(place[name] for name in axes)

    def remote(src, dst, send_sem, recv_sem, target):
        return pltpu.make_async_remote_copy(
            src_ref=src, dst_ref=dst, send_sem=send_sem, recv_sem=recv_sem,
            device_id=target, device_id_type=MESH,
        )

    def raw_copy(piece):
        part = pl.ds(pl.multiple_of(piece * PIECE * frame, PIECE * frame), PIECE * frame)
        return pltpu.make_async_copy(raw_ref.at[:, part], xbuf.at[:, part], raw_sem.at[piece])

    def history_copy():
        size = history.shape[1]
        last = raw_ref.at[:, pl.ds(spec * frame - size, size)]
        return remote(last, history, hist_send, hist_recv, peer(1, 0))

    barrier = pltpu.get_barrier_semaphore()
    senders = [(off, 0) for off in range(1, slabs)] + [(0, off) for off in range(1, owner_count)]
    if slabs > 1:
        senders += [(slabs - 1, off) for off in range(1, owner_count)]
    for slab, owner in senders:
        pl.semaphore_signal(barrier, inc=1, device_id=peer(slab, owner), device_id_type=MESH)

    constants = [
        pltpu.make_async_copy(src, dst, const_sem.at[n])
        for n, (src, dst) in enumerate(
            [
                (w1_any, w1_ref), (tw_any, tw_ref), (w2_any, w2_ref), (m_any, m_ref),
                (delays_any, delays_ref), (widths_any, widths_ref), (owners_any, owners_ref),
            ]
        )
    ]
    taps = [
        pltpu.make_async_copy(proto_ref.at[tap : tap + 1], proto.at[tap], proto_sem.at[tap])
        for tap in range(4)
    ]
    raw_copy(0).start()
    for copy in taps:
        copy.start()
    constants[0].start()
    constants[1].start()
    constants[2].start()
    raw_copy(1).start()
    for copy in constants[3:]:
        copy.start()
    for piece in range(2, spec // PIECE):
        raw_copy(piece).start()
    band_ref[...] = jnp.zeros_like(band_ref)

    def unfold(ref, start):
        return ref[:, pl.ds(start, frame)].reshape(SIDE, SIDE).astype(F32)

    def fill(base, k):
        start = pl.multiple_of((base + k) * frame, frame)
        row = pl.multiple_of((base + k + 3) * SIDE, SIDE)
        win[pl.ds(row, SIDE)] = unfold(xbuf, start)

    def pair(base, s):
        ys = []
        for k in (s, s + 1):
            acc = 0.0
            for tap in range(4):
                row = pl.multiple_of((base + k + tap) * SIDE, SIDE)
                acc = acc + win[pl.ds(row, SIDE)] * proto[tap].reshape(SIDE, SIDE)
            ys.append(acc.astype(BF16))
        a = jnp.dot(w1_ref[...], jnp.concatenate(ys, 1), preferred_element_type=F32)
        res, ims = [], []
        for m in range(2):
            re = a[:FR, m * SIDE : (m + 1) * SIDE]
            im = a[FR:, m * SIDE : (m + 1) * SIDE]
            res.append(re * tw_ref[0] - im * tw_ref[1])
            ims.append(im * tw_ref[0] + re * tw_ref[1])
        t = jnp.concatenate(
            [jnp.concatenate(res, 0).astype(BF16), jnp.concatenate(ims, 0).astype(BF16)], 1
        )
        c = jnp.dot(t, w2_ref[...], preferred_element_type=F32)
        re, im = c[:, :SIDE], c[:, SIDE:]
        power = re * re + im * im
        p_ref[pl.ds(pl.multiple_of((base + s) * FR, FR), 2 * FR)] = power
        band_ref[...] += power[:FR] + power[FR:]

    raw_copy(0).wait()
    for copy in taps:
        copy.wait()
    for copy in constants[:3]:
        copy.wait()
    for k in range(PIECE):
        fill(0, k)
    for s in range(FIRST, PIECE, 2):
        pair(0, s)
    raw_copy(1).wait()
    for k in range(PIECE, SPB):
        fill(0, k)
    for s in range(PIECE, SPB, 2):
        pair(0, s)

    pl.semaphore_wait(barrier, len(senders))
    if slabs > 1:
        history_copy().start()

    def chunk(step, carry):
        base = step * SPB
        for piece in range(SPB // PIECE):
            raw_copy(step * (SPB // PIECE) + piece).wait()
        for k in range(SPB):
            fill(base, k)
        for s in range(0, SPB, 2):
            pair(base, s)
        return carry

    lax.fori_loop(1, spec // SPB, chunk, 0)

    if slabs > 1:
        history_copy().wait()
        for k in range(3):
            win[k * SIDE : (k + 1) * SIDE] = jnp.where(tm > 0, unfold(history, k * frame), 0.0)
    else:
        win[: 3 * SIDE] = jnp.zeros((3 * SIDE, SIDE), F32)
    for s in range(0, FIRST, 2):
        pair(0, s)

    copies = []
    for off in range(1, slabs):
        copy = remote(band_ref, bands.at[off - 1], band_send.at[off - 1], band_recv.at[off - 1], peer(off, 0))
        copy.start()
        copies.append(copy)

    for copy in constants[3:]:
        copy.wait()
    lanes = (MAXT + 1) * quad
    spot = iota((NBLK, SIDE), 0)
    lane = iota((NBLK, SIDE), 1) // 2
    spread = jnp.concatenate([lane == spot, lane == NBLK - 1 - spot], 1).astype(F32).astype(BF16)
    late = jnp.dot(delays_ref[...].astype(F32).astype(BF16), spread, preferred_element_type=F32)
    line = iota((quad, 2 * SIDE), 0) // trials
    masks = [
        jnp.concatenate(
            [
                jnp.where((late == float(v)) & (line == g), 1.0, 0.0)
                for v in range(MAXT + 1)
            ],
            0,
        ).astype(BF16)
        for g in range(groups)
    ]

    def column(ref):
        n = ref.shape[1]
        same = iota((n, n), 0) == iota((n, n), 1)
        return jnp.sum(jnp.where(same, jnp.broadcast_to(ref[...], (n, n)), 0), 1, keepdims=True)

    lane = iota((groups, lanes), 1) % quad
    row = iota((groups, lanes), 0)
    owner = jnp.broadcast_to(column(owners_ref), (groups, lanes))
    mine = jnp.sum(jnp.where(lane // trials == row, owner, 0), 0, keepdims=True)
    rank = jnp.sum(jnp.where((owner == mine) & (row < lane // trials), 1, 0), 0, keepdims=True)
    place = (mine * slots + rank) * trials + lane[:1] % trials
    pack = jnp.where(iota((owner_count * rows, lanes), 0) == place, 1.0, 0.0)
    pack = jnp.concatenate([pack, pack], 1).astype(BF16)

    reach = jnp.broadcast_to(column(widths_ref), (boxes, SIDE))
    root = 1.0 / jnp.sqrt(reach.astype(F32))
    root = jnp.concatenate([root] * rows, 0)
    reach = jnp.concatenate([reach] * rows, 0)
    if WMAX * rows > SIDE:
        reach = jnp.broadcast_to(reach[:, :1], (boxes * rows, WMAX * rows))
    lag = iota((boxes * rows, WMAX * rows), 1)
    series = iota((boxes * rows, WMAX * rows), 0) // boxes
    kernel = jnp.where((lag % rows == series) & (lag // rows < reach), 1.0, 0.0)
    kernel = jnp.concatenate([kernel, kernel], 1).astype(BF16)
    direct[spec + FD - 1 :] = jnp.zeros((direct.shape[0] - spec - FD + 1, groups, SIDE), F32)
    mirror[spec + FD - 1 :] = jnp.zeros((direct.shape[0] - spec - FD + 1, groups, SIDE), F32)

    band = band_ref[...]
    for off in range(1, slabs):
        copies[off - 1].wait()
        band = band + bands[off - 1]
    scale = 1.0 / (4 * frame)
    held = iota((FR, SIDE), 0) <= HALF
    inv[...] = jnp.where(held, scale / (band * (scale / spectra) + 1e-06), 0.0)

    even = iota((FD * groups, SIDE), 1) % 2 == 0
    size = FD * groups

    def block(step, carry):
        carry = list(carry)
        for s in range(0, SPB, 2):
            flats = []
            for k in (s, s + 1):
                start = pl.multiple_of((step * SPB + k) * FR, FR)
                ratio = p_ref[pl.ds(start, FR)] * inv[...]
                total = 2.0 * jnp.sum(ratio, 0, keepdims=True) - ratio[:1] - ratio[HALF : HALF + 1]
                mean = jnp.sum(total, 1, keepdims=True) * (1.0 / frame)
                flats.append((ratio - mean).astype(BF16))
            r = jnp.dot(m_ref[...], jnp.concatenate(flats, 1), preferred_element_type=F32)
            for m in range(2):
                part = r[:, m * SIDE : (m + 1) * SIDE]
                one = jnp.where(even, part[:size], part[size : 2 * size])
                two = jnp.where(even, part[3 * size :], part[2 * size : 3 * size])
                for n, (ref, new) in enumerate(((direct, one), (mirror, two))):
                    new = [new[d * groups : (d + 1) * groups] for d in range(FD)]
                    held = carry[n * (FD - 1) : (n + 1) * (FD - 1)] + [0.0]
                    ref[step * SPB + s + m] = held[0] + new[0]
                    for d in range(1, FD):
                        carry[n * (FD - 1) + d - 1] = held[d] + new[d]
        return tuple(carry)

    zero = jnp.zeros((groups, SIDE), F32)
    carry = lax.fori_loop(0, spec // SPB, block, (zero,) * (2 * (FD - 1)))
    for d in range(FD - 1):
        direct[spec + d] = carry[d]
        mirror[spec + d] = carry[FD - 1 + d]

    count = direct.shape[0]
    each = 0.0
    for g in range(groups):
        both = jnp.concatenate([direct[:, g, :], mirror[:, g, :]], 1).astype(BF16)
        each = each + lax.dot_general(
            both, masks[g], (((1,), (1,)), ((), ())), preferred_element_type=F32
        )
    length = count + MAXT * TT
    value = iota((length, lanes), 1) // quad
    dd = 0.0
    for v in range(MAXT + 1):
        pads = [jnp.zeros((v * TT, lanes), F32), each, jnp.zeros(((MAXT - v) * TT, lanes), F32)]
        moved = jnp.concatenate([part for part in pads if part.shape[0]], 0)
        dd = jnp.where(value == v, moved, dd)
    dd = dd * (1.0 / math.sqrt(SIDE * SIDE // NBLK) / math.sqrt(NBLK))
    back = spec - TT
    dd = jnp.concatenate([dd[:spec], dd[back:], jnp.zeros((SIDE - length + back, lanes), F32)], 0)
    high = dd.astype(BF16)
    low = (dd - high.astype(F32)).astype(BF16)
    packed = lax.dot_general(
        pack, jnp.concatenate([high, low], 1), (((1,), (1,)), ((), ())), preferred_element_type=F32
    )
    send[...] = packed[:, :spec].reshape(send.shape)
    sendb[...] = packed[:, spec:].reshape(sendb.shape)

    copies = []
    for off in range(1, owner_count):
        copy = remote(
            send.at[lax.rem(dm + off, owner_count)], got.at[dm],
            own_send.at[off - 1], own_recv.at[off - 1], peer(0, off),
        )
        copy.start()
        copies.append(copy)
    if slabs > 1:
        for off in range(owner_count):
            copy = remote(
                sendb.at[lax.rem(dm + off, owner_count)], gotb.at[dm],
                next_send.at[off], next_recv.at[off], peer(1, off),
            )
            copy.start()
            copies.append(copy)
    got[dm] = send[dm]
    for copy in copies:
        copy.wait()

    lane = iota((rows, SIDE), 1)
    stacks = []
    for d in range(owner_count):
        own = got[d]
        if slabs > 1:
            before = jnp.where(tm > 0, gotb[d], 0.0)
            own = own + jnp.where(lane < SIDE - TT, pltpu.roll(before, SIDE - TT, 1), 0.0)
            past = pltpu.roll(before, SIDE - TT, 1)
        else:
            past = jnp.zeros((rows, SIDE), F32)
        moved = [own]
        for lag in range(1, WMAX):
            moved.append(jnp.where(lane < lag, pltpu.roll(past, lag, 1), pltpu.roll(own, lag, 1)))
        stacks.append(jnp.concatenate(moved, 0))
    stack = jnp.concatenate(stacks, 1)
    high = stack.astype(BF16)
    low = (stack - high.astype(F32)).astype(BF16)
    box = jnp.dot(kernel, jnp.concatenate([high, low], 0), preferred_element_type=F32)
    for d in range(owner_count):
        done = (box[:, d * SIDE : (d + 1) * SIDE] * root).astype(BF16)
        for s in range(slots):
            out_ref[s, d] = done[s * trials * boxes : (s + 1) * trials * boxes]


def shards(axes, raw, proto, delays, widths, owners):
    taps, channels = proto.shape
    spec = raw.shape[1] // channels
    groups, trials, _ = delays.shape
    slabs, owner_count = lax.axis_size("tm"), lax.axis_size("dm")
    capacity = 2 * (groups // owner_count)
    w1, w2, tw = tables(channels)
    masks = fine_rows(groups, channels // NBLK)
    sizes = (spec * slabs, spec, groups, slabs, owner_count, axes)
    rows = -(-(spec + FD - 1) // 8) * 8
    block = pltpu.VMEM((owner_count, capacity * trials, SIDE), F32)
    sems = lambda n: pltpu.SemaphoreType.DMA((max(n, 1),))
    small = [w1, w2, tw, masks, delays.reshape(groups * trials, NBLK), widths[None], owners.T]
    out = (capacity, owner_count, trials * widths.shape[0], spec)
    box = pl.pallas_call(
        functools.partial(search_kernel, sizes),
        in_specs=[pl.BlockSpec(memory_space=pl.ANY)] * (2 + len(small)),
        out_specs=pl.BlockSpec(memory_space=pltpu.VMEM),
        out_shape=jax.ShapeDtypeStruct(out, BF16),
        scratch_shapes=[
            pltpu.VMEM((1, spec * channels), BF16),
            pltpu.VMEM((taps, 1, channels), F32),
            *[pltpu.VMEM(value.shape, value.dtype) for value in small],
            pltpu.VMEM(((spec + 3) * SIDE, SIDE), F32),
            pltpu.VMEM((1, 3 * channels), BF16),
            pltpu.VMEM((spec * FR, SIDE), F32),
            pltpu.VMEM((FR, SIDE), F32),
            pltpu.VMEM((max(slabs - 1, 1), FR, SIDE), F32),
            pltpu.VMEM((FR, SIDE), F32),
            pltpu.VMEM((rows, groups, SIDE), F32),
            pltpu.VMEM((rows, groups, SIDE), F32),
            block,
            block,
            block,
            block,
            sems(spec // PIECE),
            sems(taps),
            sems(len(small)),
            pltpu.SemaphoreType.DMA,
            pltpu.SemaphoreType.DMA,
            sems(slabs - 1),
            sems(slabs - 1),
            sems(owner_count - 1),
            sems(owner_count - 1),
            sems(owner_count),
            sems(owner_count),
        ],
        compiler_params=pltpu.CompilerParams(
            vmem_limit_bytes=56 << 20, collective_id=0, has_side_effects=True
        ),
        name="search",
    )(raw, proto, *small)
    return box.reshape(capacity, owner_count, 1, trials, widths.shape[0], spec)


def solution(mesh):
    return jax.shard_map(
        functools.partial(shards, mesh.axis_names),
        mesh=mesh,
        in_specs=(P(("group", "dm", "beam"), "tm"), P(), P(), P(), P()),
        out_specs=P("dm", "group", "beam", None, None, "tm"),
        check_vma=False,
    )
```

time: 29.9 us -> 28.2 us (0.943)
  Pallas kernels: 28.2 us -> 26.5 us
    pallas_call x1, Pallas kernels: 28.2 us -> 26.5 us  [shards(): pl.pallas_call(functools.partial(search_kernel, sizes), in_specs=[pl.Bloc...]
where the time goes in v1:
time: 28.2 us; the launch traced here: 28.1 us
  Pallas kernels  26.5 us (94%)
  local copies, waits for them, and re-layouts  1.57 us (6%)
    pallas_call x1, Pallas kernels, shards(): pl.pallas_call(functools.partial(search_kernel, sizes), in_specs=[pl.Bloc...  26.5 us
    unnamed x1, local copies, waits for them, and re-layouts  1.57 us

profile of v1, /device:TPU:0, one launch (start us, length us, event | category | flops | bytes accessed | tf_op | source)
XLA Modules:
  0.0 28.1 jit_solution(5761391730172807951)
XLA Ops:
  0.0 26.5 %search.1 = bf16[4,4,32,128]{3,2,1,0:T(8,128)(2,1)} custom-call(bf16[1,2097152]{1,0:T(2,128)(2,1)} %raw_ref.1, f32[4,16384]{1,0:T(4,128)} %proto_ref.1, bf16[144,128]{1,0:T(8,128)(2,1)} %constant.8.clone.w1_any, bf16[256,256]{1,0:T(8,128)(2,1)} %constant.9.clone.w2_any, f32[2,72,128]{2,1,0:T(8,128)} %constant.10.clone.tw_any, ...), custom_call_target="tpu_custom_call" | custom-call | tf_op jit(solution)/shard_map/search/pallas_call | solution.py:373
  26.5 1.6 %copy.12 = bf16[4,4,1,4,8,128]{5,4,3,2,1,0:T(8,128)(2,1)} copy(bf16[4,4,1,4,8,128]{5,4,3,2,1,0:T(8,128)(2,1)} %bitcast.6) | data formatting | bytes 262144

commit v2 on v1

--- a/solution.py
+++ b/solution.py
@@ -17,13 +17,15 @@
 WMAX = 8
 SPB = 32
 FIRST = 4
-PIECE = 16
+CHUNK = 16
+GROUP = 4
 HALF = SIDE // 2
 FR = 72
 BACK = 128 - TT
 MESH = pl.DeviceIdType.MESH
 F32 = jnp.float32
 BF16 = jnp.bfloat16
+FT = BF16
 
 
 def tables(channels):
@@ -56,7 +58,7 @@
 def search_kernel(
     sizes, raw_ref, proto_ref, w1_any, w2_any, tw_any, m_any, delays_any, widths_any, owners_any, out_ref,
     xbuf, proto, w1_ref, w2_ref, tw_ref, m_ref, delays_ref, widths_ref, owners_ref,
-    win, history, p_ref, band_ref, bands, inv, direct, mirror, send, sendb, got, gotb,
+    yone, ytwo, history, p_ref, band_ref, bands, inv, direct, mirror, send, sendb, got, gotb,
     raw_sem, proto_sem, const_sem,
     hist_send, hist_recv, band_send, band_recv, own_send, own_recv, next_send, next_recv,
 ):
@@ -82,8 +84,12 @@
         )
 
     def raw_copy(piece):
-        part = pl.ds(pl.multiple_of(piece * PIECE * frame, PIECE * frame), PIECE * frame)
-        return pltpu.make_async_copy(raw_ref.at[:, part], xbuf.at[:, part], raw_sem.at[piece])
+        start = pl.multiple_of(piece * CHUNK * frame, CHUNK * frame)
+        return pltpu.make_async_copy(
+            raw_ref.at[:, pl.ds(start, CHUNK * frame)],
+            xbuf.at[:, pl.ds(start + 3 * frame, CHUNK * frame)],
+            raw_sem.at[piece],
+        )
 
     def history_copy():
         size = history.shape[1]
@@ -119,81 +125,95 @@
     raw_copy(1).start()
     for copy in constants[3:]:
         copy.start()
-    for piece in range(2, spec // PIECE):
+    for piece in range(2, spec // CHUNK):
         raw_copy(piece).start()
     band_ref[...] = jnp.zeros_like(band_ref)
 
-    def unfold(ref, start):
-        return ref[:, pl.ds(start, frame)].reshape(SIDE, SIDE).astype(F32)
-
-    def fill(base, k):
-        start = pl.multiple_of((base + k) * frame, frame)
-        row = pl.multiple_of((base + k + 3) * SIDE, SIDE)
-        win[pl.ds(row, SIDE)] = unfold(xbuf, start)
-
-    def pair(base, s):
-        ys = []
-        for k in (s, s + 1):
-            acc = 0.0
-            for tap in range(4):
-                row = pl.multiple_of((base + k + tap) * SIDE, SIDE)
-                acc = acc + win[pl.ds(row, SIDE)] * proto[tap].reshape(SIDE, SIDE)
-            ys.append(acc.astype(BF16))
-        a = jnp.dot(w1_ref[...], jnp.concatenate(ys, 1), preferred_element_type=F32)
-        res, ims = [], []
-        for m in range(2):
-            re = a[:FR, m * SIDE : (m + 1) * SIDE]
-            im = a[FR:, m * SIDE : (m + 1) * SIDE]
-            res.append(re * tw_ref[0] - im * tw_ref[1])
-            ims.append(im * tw_ref[0] + re * tw_ref[1])
-        t = jnp.concatenate(
-            [jnp.concatenate(res, 0).astype(BF16), jnp.concatenate(ims, 0).astype(BF16)], 1
-        )
-        c = jnp.dot(t, w2_ref[...], preferred_element_type=F32)
+    tile = 16 * SIDE
+
+    def fir(ybuf, base, tiles, first=0):
+        for r in tiles:
+            taps = [proto[tap, :, r * tile : (r + 1) * tile].reshape(16, SIDE).astype(FT) for tap in range(4)]
+            seen = []
+            for k in range(-3, CHUNK):
+                if first and k < 0:
+                    seen.append(jnp.zeros((16, SIDE), FT))
+                    continue
+                start = pl.multiple_of((base + k + 3) * frame + r * tile, tile)
+                seen.append(xbuf[:, pl.ds(start, tile)].reshape(16, SIDE).astype(FT))
+                if k >= 0:
+                    acc = (seen[k] * taps[0] + seen[k + 1] * taps[1]) + (seen[k + 2] * taps[2] + seen[k + 3] * taps[3])
+                    ybuf[k // 2, r * 16 : (r + 1) * 16, k % 2 * SIDE : (k % 2 + 1) * SIDE] = acc.astype(BF16)
+
+    def dots(ybuf, base, s, count, keep=None):
+        ts = []
+        for p in range(s // 2, s // 2 + count):
+            a = jnp.dot(w1_ref[...], ybuf[p], preferred_element_type=F32)
+            res, ims = [], []
+            for m in range(2):
+                re = a[:FR, m * SIDE : (m + 1) * SIDE]
+                im = a[FR:, m * SIDE : (m + 1) * SIDE]
+                res.append(re * tw_ref[0] - im * tw_ref[1])
+                ims.append(im * tw_ref[0] + re * tw_ref[1])
+            ts.append(
+                jnp.concatenate(
+                    [jnp.concatenate(res, 0).astype(BF16), jnp.concatenate(ims, 0).astype(BF16)], 1
+                )
+            )
+        c = jnp.dot(jnp.concatenate(ts, 0), w2_ref[...], preferred_element_type=F32)
         re, im = c[:, :SIDE], c[:, SIDE:]
         power = re * re + im * im
-        p_ref[pl.ds(pl.multiple_of((base + s) * FR, FR), 2 * FR)] = power
-        band_ref[...] += power[:FR] + power[FR:]
+        p_ref[pl.ds(pl.multiple_of((base + s) * FR, FR), 2 * count * FR)] = power
+        parts = [power[k * FR : (k + 1) * FR] for k in range(2 * count)]
+        if keep is not None:
+            parts[:FIRST] = [jnp.where(keep, part, 0.0) for part in parts[:FIRST]]
+        while len(parts) > 1:
+            parts = [parts[k] + parts[k + 1] for k in range(0, len(parts), 2)]
+        band_ref[...] += parts[0]
+
+    def stage(ybuf, base, ynext, following, keep=None):
+        units = CHUNK // (2 * GROUP)
+        for u in range(units):
+            dots(ybuf, base, 2 * GROUP * u, GROUP, keep if u == 0 else None)
+            fir(ynext, following, range(8 * u // units, 8 * (u + 1) // units))
 
     raw_copy(0).wait()
     for copy in taps:
         copy.wait()
+    fir(yone, 0, range(8), 1)
     for copy in constants[:3]:
         copy.wait()
-    for k in range(PIECE):
-        fill(0, k)
-    for s in range(FIRST, PIECE, 2):
-        pair(0, s)
-    raw_copy(1).wait()
-    for k in range(PIECE, SPB):
-        fill(0, k)
-    for s in range(PIECE, SPB, 2):
-        pair(0, s)
-
-    pl.semaphore_wait(barrier, len(senders))
-    if slabs > 1:
-        history_copy().start()
 
     def chunk(step, carry):
-        base = step * SPB
-        for piece in range(SPB // PIECE):
-            raw_copy(step * (SPB // PIECE) + piece).wait()
-        for k in range(SPB):
-            fill(base, k)
-        for s in range(0, SPB, 2):
-            pair(base, s)
+        base = step * (2 * CHUNK)
+        raw_copy(2 * step + 1).wait()
+
+        @pl.when(step < steps - 1)
+        def _():
+            raw_copy(2 * step + 2).wait()
+
+        @pl.when(step == 1)
+        def _():
+            pl.semaphore_wait(barrier, len(senders))
+            if slabs > 1:
+                history_copy().start()
+
+        @pl.when(step == steps - 1)
+        def _():
+            if slabs > 1:
+                history_copy().wait()
+                xbuf[:, : 3 * frame] = jnp.where(tm > 0, history[...], 0.0)
+            else:
+                xbuf[:, : 3 * frame] = jnp.zeros((1, 3 * frame), BF16)
+
+        stage(yone, base, ytwo, base + CHUNK, step > 0)
+        following = jnp.where(step < steps - 1, base + 2 * CHUNK, 0)
+        stage(ytwo, base + CHUNK, yone, following)
         return carry
 
-    lax.fori_loop(1, spec // SPB, chunk, 0)
-
-    if slabs > 1:
-        history_copy().wait()
-        for k in range(3):
-            win[k * SIDE : (k + 1) * SIDE] = jnp.where(tm > 0, unfold(history, k * frame), 0.0)
-    else:
-        win[: 3 * SIDE] = jnp.zeros((3 * SIDE, SIDE), F32)
-    for s in range(0, FIRST, 2):
-        pair(0, s)
+    steps = spec // (2 * CHUNK)
+    lax.fori_loop(0, steps, chunk, 0)
+    dots(yone, 0, 0, FIRST // 2)
 
     copies = []
     for off in range(1, slabs):
@@ -244,8 +264,9 @@
     series = iota((boxes * rows, WMAX * rows), 0) // boxes
     kernel = jnp.where((lag % rows == series) & (lag // rows < reach), 1.0, 0.0)
     kernel = jnp.concatenate([kernel, kernel], 1).astype(BF16)
-    direct[spec + FD - 1 :] = jnp.zeros((direct.shape[0] - spec - FD + 1, groups, SIDE), F32)
-    mirror[spec + FD - 1 :] = jnp.zeros((direct.shape[0] - spec - FD + 1, groups, SIDE), F32)
+    used = (spec + FD - 1) * groups
+    direct[used:] = jnp.zeros((direct.shape[0] - used, SIDE), F32)
+    mirror[used:] = jnp.zeros((direct.shape[0] - used, SIDE), F32)
 
     band = band_ref[...]
     for off in range(1, slabs):
@@ -276,7 +297,8 @@
                 for n, (ref, new) in enumerate(((direct, one), (mirror, two))):
                     new = [new[d * groups : (d + 1) * groups] for d in range(FD)]
                     held = carry[n * (FD - 1) : (n + 1) * (FD - 1)] + [0.0]
-                    ref[step * SPB + s + m] = held[0] + new[0]
+                    at = pl.multiple_of((step * SPB + s + m) * groups, groups)
+                    ref[pl.ds(at, groups)] = held[0] + new[0]
                     for d in range(1, FD):
                         carry[n * (FD - 1) + d - 1] = held[d] + new[d]
         return tuple(carry)
@@ -284,13 +306,14 @@
     zero = jnp.zeros((groups, SIDE), F32)
     carry = lax.fori_loop(0, spec // SPB, block, (zero,) * (2 * (FD - 1)))
     for d in range(FD - 1):
-        direct[spec + d] = carry[d]
-        mirror[spec + d] = carry[FD - 1 + d]
-
-    count = direct.shape[0]
+        direct[(spec + d) * groups : (spec + d + 1) * groups] = carry[d]
+        mirror[(spec + d) * groups : (spec + d + 1) * groups] = carry[FD - 1 + d]
+
+    count = direct.shape[0] // groups
     each = 0.0
     for g in range(groups):
-        both = jnp.concatenate([direct[:, g, :], mirror[:, g, :]], 1).astype(BF16)
+        rows_g = pl.ds(g, count, stride=groups)
+        both = jnp.concatenate([direct[rows_g, :], mirror[rows_g, :]], 1).astype(BF16)
         each = each + lax.dot_general(
             both, masks[g], (((1,), (1,)), ((), ())), preferred_element_type=F32
         )
@@ -376,22 +399,23 @@
         out_specs=pl.BlockSpec(memory_space=pltpu.VMEM),
         out_shape=jax.ShapeDtypeStruct(out, BF16),
         scratch_shapes=[
-            pltpu.VMEM((1, spec * channels), BF16),
+            pltpu.VMEM((1, (spec + 3) * channels), BF16),
             pltpu.VMEM((taps, 1, channels), F32),
             *[pltpu.VMEM(value.shape, value.dtype) for value in small],
-            pltpu.VMEM(((spec + 3) * SIDE, SIDE), F32),
+            pltpu.VMEM((CHUNK // 2, SIDE, 2 * SIDE), BF16),
+            pltpu.VMEM((CHUNK // 2, SIDE, 2 * SIDE), BF16),
             pltpu.VMEM((1, 3 * channels), BF16),
             pltpu.VMEM((spec * FR, SIDE), F32),
             pltpu.VMEM((FR, SIDE), F32),
             pltpu.VMEM((max(slabs - 1, 1), FR, SIDE), F32),
             pltpu.VMEM((FR, SIDE), F32),
-            pltpu.VMEM((rows, groups, SIDE), F32),
-            pltpu.VMEM((rows, groups, SIDE), F32),
+            pltpu.VMEM((rows * groups, SIDE), F32),
+            pltpu.VMEM((rows * groups, SIDE), F32),
             block,
             block,
             block,
             block,
-            sems(spec // PIECE),
+            sems(spec // CHUNK),
             sems(taps),
             sems(len(small)),
             pltpu.SemaphoreType.DMA,

time: 28.2 us -> 29 us (1.028)
  Pallas kernels: 26.5 us -> 27.3 us
    pallas_call x1, Pallas kernels: 26.5 us -> 27.3 us  [shards(): pl.pallas_call(functools.partial(search_kernel, sizes), in_specs=[pl.Bloc...]
where the time goes in v2:
time: 29 us; the launch traced here: 28.9 us
  Pallas kernels  27.3 us (94%)
  local copies, waits for them, and re-layouts  1.57 us (5%)
    pallas_call x1, Pallas kernels, shards(): pl.pallas_call(functools.partial(search_kernel, sizes), in_specs=[pl.Bloc...  27.3 us
    unnamed x1, local copies, waits for them, and re-layouts  1.57 us

profile of v2, /device:TPU:0, one launch (start us, length us, event | category | flops | bytes accessed | tf_op | source)
XLA Modules:
  0.0 28.9 jit_solution(2542605811146219743)
XLA Ops:
  0.0 27.3 %search.1 = bf16[4,4,32,128]{3,2,1,0:T(8,128)(2,1)} custom-call(bf16[1,2097152]{1,0:T(2,128)(2,1)} %raw_ref.1, f32[4,16384]{1,0:T(4,128)} %proto_ref.1, bf16[144,128]{1,0:T(8,128)(2,1)} %constant.8.clone.w1_any, bf16[256,256]{1,0:T(8,128)(2,1)} %constant.9.clone.w2_any, f32[2,72,128]{2,1,0:T(8,128)} %constant.10.clone.tw_any, ...), custom_call_target="tpu_custom_call" | custom-call | tf_op jit(solution)/shard_map/search/pallas_call | solution.py:396
  27.3 1.6 %copy.12 = bf16[4,4,1,4,8,128]{5,4,3,2,1,0:T(8,128)(2,1)} copy(bf16[4,4,1,4,8,128]{5,4,3,2,1,0:T(8,128)(2,1)} %bitcast.6) | data formatting | bytes 262144

commit v3 on v2

--- a/solution.py
+++ b/solution.py
@@ -19,6 +19,7 @@
 FIRST = 4
 CHUNK = 16
 GROUP = 4
+AHEAD = 3
 HALF = SIDE // 2
 FR = 72
 BACK = 128 - TT
@@ -125,7 +126,7 @@
     raw_copy(1).start()
     for copy in constants[3:]:
         copy.start()
-    for piece in range(2, spec // CHUNK):
+    for piece in range(2, AHEAD):
         raw_copy(piece).start()
     band_ref[...] = jnp.zeros_like(band_ref)
 
@@ -177,26 +178,33 @@
             dots(ybuf, base, 2 * GROUP * u, GROUP, keep if u == 0 else None)
             fir(ynext, following, range(8 * u // units, 8 * (u + 1) // units))
 
+    pl.semaphore_wait(barrier, len(senders))
+    if slabs > 1:
+        history_copy().start()
     raw_copy(0).wait()
     for copy in taps:
         copy.wait()
+    raw_copy(AHEAD).start()
     fir(yone, 0, range(8), 1)
     for copy in constants[:3]:
         copy.wait()
 
     def chunk(step, carry):
         base = step * (2 * CHUNK)
-        raw_copy(2 * step + 1).wait()
-
-        @pl.when(step < steps - 1)
-        def _():
-            raw_copy(2 * step + 2).wait()
-
-        @pl.when(step == 1)
-        def _():
-            pl.semaphore_wait(barrier, len(senders))
-            if slabs > 1:
-                history_copy().start()
+
+        def arrive(piece):
+            @pl.when(piece < pieces)
+            def _():
+                raw_copy(piece).wait()
+
+            @pl.when(piece + AHEAD < pieces)
+            def _():
+                raw_copy(piece + AHEAD).start()
+
+        arrive(2 * step + 1)
+
+        stage(yone, base, ytwo, base + CHUNK, step > 0)
+        arrive(2 * step + 2)
 
         @pl.when(step == steps - 1)
         def _():
@@ -206,12 +214,12 @@
             else:
                 xbuf[:, : 3 * frame] = jnp.zeros((1, 3 * frame), BF16)
 
-        stage(yone, base, ytwo, base + CHUNK, step > 0)
         following = jnp.where(step < steps - 1, base + 2 * CHUNK, 0)
         stage(ytwo, base + CHUNK, yone, following)
         return carry
 
-    steps = spec // (2 * CHUNK)
+    pieces = spec // CHUNK
+    steps = pieces // 2
     lax.fori_loop(0, steps, chunk, 0)
     dots(yone, 0, 0, FIRST // 2)
 
@@ -397,7 +405,7 @@
         functools.partial(search_kernel, sizes),
         in_specs=[pl.BlockSpec(memory_space=pl.ANY)] * (2 + len(small)),
         out_specs=pl.BlockSpec(memory_space=pltpu.VMEM),
-        out_shape=jax.ShapeDtypeStruct(out, BF16),
+        out_shape=pltpu.VMEM(out, BF16),
         scratch_shapes=[
             pltpu.VMEM((1, (spec + 3) * channels), BF16),
             pltpu.VMEM((taps, 1, channels), F32),

time: 29 us -> 23 us (0.79)
  Pallas kernels: 27.3 us -> 22.2 us
  local copies, waits for them, and re-layouts: 1.57 us -> 0.66 us
    pallas_call x1, Pallas kernels: 27.3 us -> 22.2 us  [shards(): pl.pallas_call(functools.partial(search_kernel, sizes), in_specs=[pl.Bloc...]
    unnamed x1, local copies, waits for them, and re-layouts: 1.57 us -> 0.66 us
where the time goes in v3:
time: 23 us; the launch traced here: 22.9 us
  Pallas kernels  22.2 us (97%)
  local copies, waits for them, and re-layouts  0.66 us (3%)
    pallas_call x1, Pallas kernels, shards(): pl.pallas_call(functools.partial(search_kernel, sizes), in_specs=[pl.Bloc...  22.2 us
    unnamed x1, local copies, waits for them, and re-layouts  0.66 us

profile of v3, /device:TPU:0, one launch (start us, length us, event | category | flops | bytes accessed | tf_op | source)
XLA Modules:
  0.0 22.9 jit_solution(5239317970319504856)
XLA Ops:
  0.0 22.2 %search.1 = bf16[4,4,32,128]{3,2,1,0:T(8,128)(2,1)S(1)} custom-call(bf16[1,2097152]{1,0:T(2,128)(2,1)} %raw_ref.1, f32[4,16384]{1,0:T(4,128)} %proto_ref.1, bf16[144,128]{1,0:T(8,128)(2,1)} %constant.8.clone.w1_any, bf16[256,256]{1,0:T(8,128)(2,1)} %constant.9.clone.w2_any, f32[2,72,128]{2,1,0:T(8,128)} %constant.10.clone.tw_any, ...), custom_call_target="tpu_custom_call" | custom-call | tf_op jit(solution)/shard_map/search/pallas_call | solution.py:404
  22.2 0.7 %copy.12 = bf16[4,4,1,4,8,128]{5,4,3,2,1,0:T(8,128)(2,1)} copy(bf16[4,4,1,4,8,128]{5,4,3,2,1,0:T(8,128)(2,1)S(1)} %bitcast.6) | data formatting | bytes 262144

commit v4 on v3

--- a/solution.py
+++ b/solution.py
@@ -15,7 +15,7 @@
 TT = 8
 MAXT = 3
 WMAX = 8
-SPB = 32
+SPB = 64
 FIRST = 4
 CHUNK = 16
 GROUP = 4
@@ -129,17 +129,15 @@
     for piece in range(2, AHEAD):
         raw_copy(piece).start()
     band_ref[...] = jnp.zeros_like(band_ref)
+    xbuf[:, : 3 * frame] = jnp.zeros((1, 3 * frame), BF16)
 
     tile = 16 * SIDE
 
-    def fir(ybuf, base, tiles, first=0):
+    def fir(ybuf, base, tiles, count=CHUNK):
         for r in tiles:
             taps = [proto[tap, :, r * tile : (r + 1) * tile].reshape(16, SIDE).astype(FT) for tap in range(4)]
             seen = []
-            for k in range(-3, CHUNK):
-                if first and k < 0:
-                    seen.append(jnp.zeros((16, SIDE), FT))
-                    continue
+            for k in range(-3, count):
                 start = pl.multiple_of((base + k + 3) * frame + r * tile, tile)
                 seen.append(xbuf[:, pl.ds(start, tile)].reshape(16, SIDE).astype(FT))
                 if k >= 0:
@@ -185,7 +183,7 @@
     for copy in taps:
         copy.wait()
     raw_copy(AHEAD).start()
-    fir(yone, 0, range(8), 1)
+    fir(yone, 0, range(8))
     for copy in constants[:3]:
         copy.wait()
 
@@ -202,18 +200,9 @@
                 raw_copy(piece + AHEAD).start()
 
         arrive(2 * step + 1)
+        arrive(2 * step + 2)
 
         stage(yone, base, ytwo, base + CHUNK, step > 0)
-        arrive(2 * step + 2)
-
-        @pl.when(step == steps - 1)
-        def _():
-            if slabs > 1:
-                history_copy().wait()
-                xbuf[:, : 3 * frame] = jnp.where(tm > 0, history[...], 0.0)
-            else:
-                xbuf[:, : 3 * frame] = jnp.zeros((1, 3 * frame), BF16)
-
         following = jnp.where(step < steps - 1, base + 2 * CHUNK, 0)
         stage(ytwo, base + CHUNK, yone, following)
         return carry
@@ -221,6 +210,10 @@
     pieces = spec // CHUNK
     steps = pieces // 2
     lax.fori_loop(0, steps, chunk, 0)
+    if slabs > 1:
+        history_copy().wait()
+        xbuf[:, : 3 * frame] = jnp.where(tm > 0, history[...], 0.0)
+        fir(yone, 0, range(8), FIRST)
     dots(yone, 0, 0, FIRST // 2)
 
     copies = []
@@ -287,17 +280,17 @@
     even = iota((FD * groups, SIDE), 1) % 2 == 0
     size = FD * groups
 
+    def flat(step, k):
+        ratio = p_ref[pl.ds(pl.multiple_of((step * SPB + k) * FR, FR), FR)] * inv[...]
+        total = 2.0 * jnp.sum(ratio, 0, keepdims=True) - ratio[:1] - ratio[HALF : HALF + 1]
+        mean = jnp.sum(total, 1, keepdims=True) * (1.0 / frame)
+        return (ratio - mean).astype(BF16)
+
     def block(step, carry):
         carry = list(carry)
         for s in range(0, SPB, 2):
-            flats = []
-            for k in (s, s + 1):
-                start = pl.multiple_of((step * SPB + k) * FR, FR)
-                ratio = p_ref[pl.ds(start, FR)] * inv[...]
-                total = 2.0 * jnp.sum(ratio, 0, keepdims=True) - ratio[:1] - ratio[HALF : HALF + 1]
-                mean = jnp.sum(total, 1, keepdims=True) * (1.0 / frame)
-                flats.append((ratio - mean).astype(BF16))
-            r = jnp.dot(m_ref[...], jnp.concatenate(flats, 1), preferred_element_type=F32)
+            flats = jnp.concatenate([flat(step, s), flat(step, s + 1)], 1)
+            r = jnp.dot(m_ref[...], flats, preferred_element_type=F32)
             for m in range(2):
                 part = r[:, m * SIDE : (m + 1) * SIDE]
                 one = jnp.where(even, part[:size], part[size : 2 * size])
@@ -311,39 +304,67 @@
                         carry[n * (FD - 1) + d - 1] = held[d] + new[d]
         return tuple(carry)
 
-    zero = jnp.zeros((groups, SIDE), F32)
-    carry = lax.fori_loop(0, spec // SPB, block, (zero,) * (2 * (FD - 1)))
+    def sweep(first, last):
+        zero = jnp.zeros((groups, SIDE), F32)
+        return lax.fori_loop(first, last, block, (zero,) * (2 * (FD - 1)))
+
+    def series(first, count):
+        each = 0.0
+        for g in range(groups):
+            picked = pl.ds(first * groups + g, count, stride=groups)
+            both = jnp.concatenate([direct[picked, :], mirror[picked, :]], 1).astype(BF16)
+            each = each + lax.dot_general(
+                both, masks[g], (((1,), (1,)), ((), ())), preferred_element_type=F32
+            )
+        return each * (1.0 / math.sqrt(SIDE * SIDE // NBLK) / math.sqrt(NBLK))
+
+    def gather(each, skip, count):
+        length = skip + count
+        padded = each
+        if length > each.shape[0]:
+            padded = jnp.concatenate([each, jnp.zeros((length - each.shape[0], lanes), F32)], 0)
+        value = iota((count, lanes), 1) // quad
+        dd = 0.0
+        for v in range(MAXT + 1):
+            start = skip - v * TT
+            if start < 0:
+                moved = jnp.concatenate([jnp.zeros((-start, lanes), F32), padded[: count + start]], 0)
+            else:
+                moved = padded[start : start + count]
+            dd = jnp.where(value == v, moved, dd)
+        if count < SIDE:
+            dd = jnp.concatenate([dd, jnp.zeros((SIDE - count, lanes), F32)], 0)
+        high = dd.astype(BF16)
+        low = (dd - high.astype(F32)).astype(BF16)
+        return lax.dot_general(
+            pack, jnp.concatenate([high, low], 1), (((1,), (1,)), ((), ())), preferred_element_type=F32
+        )
+
+    blocks = spec // SPB
+    middle = blocks // 2
+    count = direct.shape[0] // groups
+    carry = sweep(middle, blocks)
     for d in range(FD - 1):
         direct[(spec + d) * groups : (spec + d + 1) * groups] = carry[d]
         mirror[(spec + d) * groups : (spec + d + 1) * groups] = carry[FD - 1 + d]
-
-    count = direct.shape[0] // groups
-    each = 0.0
-    for g in range(groups):
-        rows_g = pl.ds(g, count, stride=groups)
-        both = jnp.concatenate([direct[rows_g, :], mirror[rows_g, :]], 1).astype(BF16)
-        each = each + lax.dot_general(
-            both, masks[g], (((1,), (1,)), ((), ())), preferred_element_type=F32
-        )
-    length = count + MAXT * TT
-    value = iota((length, lanes), 1) // quad
-    dd = 0.0
-    for v in range(MAXT + 1):
-        pads = [jnp.zeros((v * TT, lanes), F32), each, jnp.zeros(((MAXT - v) * TT, lanes), F32)]
-        moved = jnp.concatenate([part for part in pads if part.shape[0]], 0)
-        dd = jnp.where(value == v, moved, dd)
-    dd = dd * (1.0 / math.sqrt(SIDE * SIDE // NBLK) / math.sqrt(NBLK))
-    back = spec - TT
-    dd = jnp.concatenate([dd[:spec], dd[back:], jnp.zeros((SIDE - length + back, lanes), F32)], 0)
-    high = dd.astype(BF16)
-    low = (dd - high.astype(F32)).astype(BF16)
-    packed = lax.dot_general(
-        pack, jnp.concatenate([high, low], 1), (((1,), (1,)), ((), ())), preferred_element_type=F32
-    )
-    send[...] = packed[:, :spec].reshape(send.shape)
-    sendb[...] = packed[:, spec:].reshape(sendb.shape)
-
     copies = []
+    if slabs > 1:
+        reach = (MAXT + 1) * TT
+        late = series(spec - reach, count - spec + reach)
+        sendb[...] = gather(late, reach - TT, count - spec + reach).reshape(sendb.shape)
+        for off in range(owner_count - 1, -1, -1):
+            copy = remote(
+                sendb.at[lax.rem(dm + off, owner_count)], gotb.at[dm],
+                next_send.at[off], next_recv.at[off], peer(1, off),
+            )
+            copy.start()
+            copies.append(copy)
+    carry = sweep(0, middle)
+    for d in range(FD - 1):
+        start = (middle * SPB + d) * groups
+        direct[start : start + groups] += carry[d]
+        mirror[start : start + groups] += carry[FD - 1 + d]
+    send[...] = gather(series(0, spec), 0, spec).reshape(send.shape)
     for off in range(1, owner_count):
         copy = remote(
             send.at[lax.rem(dm + off, owner_count)], got.at[dm],
@@ -351,14 +372,6 @@
         )
         copy.start()
         copies.append(copy)
-    if slabs > 1:
-        for off in range(owner_count):
-            copy = remote(
-                sendb.at[lax.rem(dm + off, owner_count)], gotb.at[dm],
-                next_send.at[off], next_recv.at[off], peer(1, off),
-            )
-            copy.start()
-            copies.append(copy)
     got[dm] = send[dm]
     for copy in copies:
         copy.wait()

time: 23 us -> 22.8 us (level)
  Pallas kernels: 22.2 us -> 21.9 us
    pallas_call x1, Pallas kernels: 22.2 us -> 21.9 us  [shards(): pl.pallas_call(functools.partial(search_kernel, sizes), in_specs=[pl.Bloc...]
where the time goes in v4:
time: 22.8 us; the launch traced here: 22.6 us
  Pallas kernels  21.9 us (96%)
  local copies, waits for them, and re-layouts  0.66 us (3%)
    pallas_call x1, Pallas kernels, shards(): pl.pallas_call(functools.partial(search_kernel, sizes), in_specs=[pl.Bloc...  21.9 us
    unnamed x1, local copies, waits for them, and re-layouts  0.66 us

profile of v4, /device:TPU:0, one launch (start us, length us, event | category | flops | bytes accessed | tf_op | source)
XLA Modules:
  0.0 22.6 jit_solution(12920753161609775297)
XLA Ops:
  0.0 21.9 %search.1 = bf16[4,4,32,128]{3,2,1,0:T(8,128)(2,1)S(1)} custom-call(bf16[1,2097152]{1,0:T(2,128)(2,1)} %raw_ref.1, f32[4,16384]{1,0:T(4,128)} %proto_ref.1, bf16[144,128]{1,0:T(8,128)(2,1)} %constant.8.clone.w1_any, bf16[256,256]{1,0:T(8,128)(2,1)} %constant.9.clone.w2_any, f32[2,72,128]{2,1,0:T(8,128)} %constant.10.clone.tw_any, ...), custom_call_target="tpu_custom_call" | custom-call | tf_op jit(solution)/shard_map/search/pallas_call | solution.py:417
  22.0 0.7 %copy.12 = bf16[4,4,1,4,8,128]{5,4,3,2,1,0:T(8,128)(2,1)} copy(bf16[4,4,1,4,8,128]{5,4,3,2,1,0:T(8,128)(2,1)S(1)} %bitcast.6) | data formatting | bytes 262144

commit v5 on v4

--- a/solution.py
+++ b/solution.py
@@ -18,7 +18,7 @@
 SPB = 64
 FIRST = 4
 CHUNK = 16
-GROUP = 4
+GROUP = 8
 AHEAD = 3
 HALF = SIDE // 2
 FR = 72
@@ -33,11 +33,11 @@
     i = np.arange(SIDE)
     ang = (i[:, None] * i[None, :] % SIDE) * (2.0 * math.pi / SIDE)
     c, s = np.cos(ang), np.sin(ang)
-    w1 = np.concatenate([c[:FR], s[:FR]], 0)
+    w1 = np.concatenate([c[:HALF], s[:HALF], c[HALF:FR], s[HALF:FR]], 0)
     w2 = np.block([[c, -s], [-s, -c]])
     tw = (i[:, None] * i[None, :] % channels) * (2.0 * math.pi / channels)
     twiddle = np.stack([np.cos(tw[:FR]), np.sin(tw[:FR])]).astype(np.float32)
-    return jnp.asarray(w1, BF16), jnp.asarray(w2, BF16), jnp.asarray(twiddle)
+    return jnp.asarray(w1, BF16), jnp.asarray(w2, BF16), jnp.asarray(twiddle[:, :HALF], BF16), jnp.asarray(twiddle[:, HALF:])
 
 
 def fine_rows(groups, width):
@@ -57,8 +57,8 @@
 
 
 def search_kernel(
-    sizes, raw_ref, proto_ref, w1_any, w2_any, tw_any, m_any, delays_any, widths_any, owners_any, out_ref,
-    xbuf, proto, w1_ref, w2_ref, tw_ref, m_ref, delays_ref, widths_ref, owners_ref,
+    sizes, raw_ref, proto_ref, w1_any, w2_any, tw_any, last_any, m_any, delays_any, widths_any, owners_any, out_ref,
+    xbuf, proto, w1_ref, w2_ref, tw_ref, last_ref, m_ref, delays_ref, widths_ref, owners_ref,
     yone, ytwo, history, p_ref, band_ref, bands, inv, direct, mirror, send, sendb, got, gotb,
     raw_sem, proto_sem, const_sem,
     hist_send, hist_recv, band_send, band_recv, own_send, own_recv, next_send, next_recv,
@@ -108,7 +108,7 @@
         pltpu.make_async_copy(src, dst, const_sem.at[n])
         for n, (src, dst) in enumerate(
             [
-                (w1_any, w1_ref), (tw_any, tw_ref), (w2_any, w2_ref), (m_any, m_ref),
+                (w1_any, w1_ref), (tw_any, tw_ref), (last_any, last_ref), (w2_any, w2_ref), (m_any, m_ref),
                 (delays_any, delays_ref), (widths_any, widths_ref), (owners_any, owners_ref),
             ]
         )
@@ -123,8 +123,9 @@
     constants[0].start()
     constants[1].start()
     constants[2].start()
+    constants[3].start()
     raw_copy(1).start()
-    for copy in constants[3:]:
+    for copy in constants[4:]:
         copy.start()
     for piece in range(2, AHEAD):
         raw_copy(piece).start()
@@ -148,22 +149,27 @@
         ts = []
         for p in range(s // 2, s // 2 + count):
             a = jnp.dot(w1_ref[...], ybuf[p], preferred_element_type=F32)
-            res, ims = [], []
+            res, ims, tails = [], [], []
             for m in range(2):
-                re = a[:FR, m * SIDE : (m + 1) * SIDE]
-                im = a[FR:, m * SIDE : (m + 1) * SIDE]
+                part = a[:, m * SIDE : (m + 1) * SIDE]
+                re, im = part[:HALF].astype(BF16), part[HALF : 2 * HALF].astype(BF16)
                 res.append(re * tw_ref[0] - im * tw_ref[1])
                 ims.append(im * tw_ref[0] + re * tw_ref[1])
-            ts.append(
-                jnp.concatenate(
-                    [jnp.concatenate(res, 0).astype(BF16), jnp.concatenate(ims, 0).astype(BF16)], 1
-                )
-            )
+                re, im = part[2 * HALF : HALF + FR], part[HALF + FR :]
+                tails.append((re * last_ref[0] - im * last_ref[1], im * last_ref[0] + re * last_ref[1]))
+            for n, parts in enumerate((res, ims)):
+                parts.append(jnp.concatenate([tail[n] for tail in tails], 0).astype(BF16))
+            ts.append(jnp.concatenate([jnp.concatenate(res, 0), jnp.concatenate(ims, 0)], 1))
         c = jnp.dot(jnp.concatenate(ts, 0), w2_ref[...], preferred_element_type=F32)
         re, im = c[:, :SIDE], c[:, SIDE:]
         power = re * re + im * im
-        p_ref[pl.ds(pl.multiple_of((base + s) * FR, FR), 2 * count * FR)] = power
-        parts = [power[k * FR : (k + 1) * FR] for k in range(2 * count)]
+        parts = []
+        for k in range(2 * count):
+            top = k // 2 * 2 * FR
+            head = top + k % 2 * HALF
+            tail = top + 2 * HALF + k % 2 * (FR - HALF)
+            parts.append(jnp.concatenate([power[head : head + HALF], power[tail : tail + FR - HALF]], 0))
+            p_ref[pl.ds(pl.multiple_of((base + s + k) * FR, FR), FR)] = parts[-1]
         if keep is not None:
             parts[:FIRST] = [jnp.where(keep, part, 0.0) for part in parts[:FIRST]]
         while len(parts) > 1:
@@ -184,16 +190,14 @@
         copy.wait()
     raw_copy(AHEAD).start()
     fir(yone, 0, range(8))
-    for copy in constants[:3]:
+    for copy in constants[:4]:
         copy.wait()
 
     def chunk(step, carry):
         base = step * (2 * CHUNK)
 
         def arrive(piece):
-            @pl.when(piece < pieces)
-            def _():
-                raw_copy(piece).wait()
+            raw_copy(piece).wait()
 
             @pl.when(piece + AHEAD < pieces)
             def _():
@@ -203,17 +207,21 @@
         arrive(2 * step + 2)
 
         stage(yone, base, ytwo, base + CHUNK, step > 0)
-        following = jnp.where(step < steps - 1, base + 2 * CHUNK, 0)
-        stage(ytwo, base + CHUNK, yone, following)
+        stage(ytwo, base + CHUNK, yone, base + 2 * CHUNK)
         return carry
 
     pieces = spec // CHUNK
     steps = pieces // 2
-    lax.fori_loop(0, steps, chunk, 0)
+    lax.fori_loop(0, steps - 1, chunk, 0)
+    base = spec - 2 * CHUNK
+    raw_copy(pieces - 1).wait()
+    stage(yone, base, ytwo, base + CHUNK)
     if slabs > 1:
         history_copy().wait()
         xbuf[:, : 3 * frame] = jnp.where(tm > 0, history[...], 0.0)
-        fir(yone, 0, range(8), FIRST)
+    fir(yone, 0, range(8), FIRST)
+    for s in range(0, CHUNK, 2 * GROUP):
+        dots(ytwo, base + CHUNK, s, GROUP)
     dots(yone, 0, 0, FIRST // 2)
 
     copies = []
@@ -222,7 +230,7 @@
         copy.start()
         copies.append(copy)
 
-    for copy in constants[3:]:
+    for copy in constants[4:]:
         copy.wait()
     lanes = (MAXT + 1) * quad
     spot = iota((NBLK, SIDE), 0)
@@ -381,14 +389,13 @@
     for d in range(owner_count):
         own = got[d]
         if slabs > 1:
-            before = jnp.where(tm > 0, gotb[d], 0.0)
-            own = own + jnp.where(lane < SIDE - TT, pltpu.roll(before, SIDE - TT, 1), 0.0)
-            past = pltpu.roll(before, SIDE - TT, 1)
+            past = pltpu.roll(jnp.where(tm > 0, gotb[d], 0.0), SIDE - TT, 1)
+            own = own + jnp.where(lane < SIDE - TT, past, 0.0)
         else:
             past = jnp.zeros((rows, SIDE), F32)
         moved = [own]
         for lag in range(1, WMAX):
-            moved.append(jnp.where(lane < lag, pltpu.roll(past, lag, 1), pltpu.roll(own, lag, 1)))
+            moved.append(pltpu.roll(jnp.where(lane < SIDE - lag, own, past), lag, 1))
         stacks.append(jnp.concatenate(moved, 0))
     stack = jnp.concatenate(stacks, 1)
     high = stack.astype(BF16)
@@ -406,13 +413,13 @@
     groups, trials, _ = delays.shape
     slabs, owner_count = lax.axis_size("tm"), lax.axis_size("dm")
     capacity = 2 * (groups // owner_count)
-    w1, w2, tw = tables(channels)
+    w1, w2, tw, last = tables(channels)
     masks = fine_rows(groups, channels // NBLK)
     sizes = (spec * slabs, spec, groups, slabs, owner_count, axes)
     rows = -(-(spec + FD - 1) // 8) * 8
     block = pltpu.VMEM((owner_count, capacity * trials, SIDE), F32)
     sems = lambda n: pltpu.SemaphoreType.DMA((max(n, 1),))
-    small = [w1, w2, tw, masks, delays.reshape(groups * trials, NBLK), widths[None], owners.T]
+    small = [w1, w2, tw, last, masks, delays.reshape(groups * trials, NBLK), widths[None], owners.T]
     out = (capacity, owner_count, trials * widths.shape[0], spec)
     box = pl.pallas_call(
         functools.partial(search_kernel, sizes),

time: 22.8 us -> 22.2 us (0.974)
  Pallas kernels: 21.9 us -> 21.4 us
    pallas_call x1, Pallas kernels: 21.9 us -> 21.4 us  [shards(): pl.pallas_call(functools.partial(search_kernel, sizes), in_specs=[pl.Bloc...]
where the time goes in v5:
time: 22.2 us; the launch traced here: 22 us
  Pallas kernels  21.4 us (96%)
  local copies, waits for them, and re-layouts  0.66 us (3%)
    pallas_call x1, Pallas kernels, shards(): pl.pallas_call(functools.partial(search_kernel, sizes), in_specs=[pl.Bloc...  21.4 us
    unnamed x1, local copies, waits for them, and re-layouts  0.66 us

profile of v5, /device:TPU:0, one launch (start us, length us, event | category | flops | bytes accessed | tf_op | source)
XLA Modules:
  0.0 22.0 jit_solution(9941309532130591790)
XLA Ops:
  0.0 21.4 %search.1 = bf16[4,4,32,128]{3,2,1,0:T(8,128)(2,1)S(1)} custom-call(bf16[1,2097152]{1,0:T(2,128)(2,1)} %raw_ref.1, f32[4,16384]{1,0:T(4,128)} %proto_ref.1, bf16[144,128]{1,0:T(8,128)(2,1)} %constant.10.clone.w1_any, bf16[256,256]{1,0:T(8,128)(2,1)} %constant.11.clone.w2_any, bf16[2,64,128]{2,1,0:T(8,128)(2,1)} %constant.12.clone.tw_any, ...), custom_call_target="tpu_custom_call" | custom-call | tf_op jit(solution)/shard_map/search/pallas_call | solution.py:424
  21.4 0.7 %copy.13 = bf16[4,4,1,4,8,128]{5,4,3,2,1,0:T(8,128)(2,1)} copy(bf16[4,4,1,4,8,128]{5,4,3,2,1,0:T(8,128)(2,1)S(1)} %bitcast.6) | data formatting | bytes 262144

commit v6 on v5

--- a/solution.py
+++ b/solution.py
@@ -22,6 +22,7 @@
 AHEAD = 3
 HALF = SIDE // 2
 FR = 72
+FS = 80
 BACK = 128 - TT
 MESH = pl.DeviceIdType.MESH
 F32 = jnp.float32
@@ -59,8 +60,8 @@
 def search_kernel(
     sizes, raw_ref, proto_ref, w1_any, w2_any, tw_any, last_any, m_any, delays_any, widths_any, owners_any, out_ref,
     xbuf, proto, w1_ref, w2_ref, tw_ref, last_ref, m_ref, delays_ref, widths_ref, owners_ref,
-    yone, ytwo, history, p_ref, band_ref, bands, inv, direct, mirror, send, sendb, got, gotb,
-    raw_sem, proto_sem, const_sem,
+    yone, ytwo, history, p_ref, band_ref, band_out, bands, inv, direct, mirror, send, sendb, got, gotb,
+    masks, pack_ref, kernel_ref, root_ref, open_sem, raw_sem, proto_sem, const_sem,
     hist_send, hist_recv, band_send, band_recv, own_send, own_recv, next_send, next_recv,
 ):
     spectra, spec, groups, slabs, owner_count, axes = sizes
@@ -92,11 +93,27 @@
             raw_sem.at[piece],
         )
 
+    def opening(half):
+        start = half * CHUNK // 2 * frame
+        return pltpu.make_async_copy(
+            raw_ref.at[:, pl.ds(start, CHUNK // 2 * frame)],
+            xbuf.at[:, pl.ds(start + 3 * frame, CHUNK // 2 * frame)],
+            open_sem.at[half],
+        )
+
     def history_copy():
         size = history.shape[1]
         last = raw_ref.at[:, pl.ds(spec * frame - size, size)]
         return remote(last, history, hist_send, hist_recv, peer(1, 0))
 
+    taps = [
+        pltpu.make_async_copy(proto_ref.at[tap : tap + 1], proto.at[tap], proto_sem.at[tap])
+        for tap in range(4)
+    ]
+    opening(0).start()
+    for copy in taps:
+        copy.start()
+    opening(1).start()
     barrier = pltpu.get_barrier_semaphore()
     senders = [(off, 0) for off in range(1, slabs)] + [(0, off) for off in range(1, owner_count)]
     if slabs > 1:
@@ -113,13 +130,6 @@
             ]
         )
     ]
-    taps = [
-        pltpu.make_async_copy(proto_ref.at[tap : tap + 1], proto.at[tap], proto_sem.at[tap])
-        for tap in range(4)
-    ]
-    raw_copy(0).start()
-    for copy in taps:
-        copy.start()
     constants[0].start()
     constants[1].start()
     constants[2].start()
@@ -134,15 +144,15 @@
 
     tile = 16 * SIDE
 
-    def fir(ybuf, base, tiles, count=CHUNK):
+    def fir(ybuf, base, tiles, first=0, last=CHUNK):
         for r in tiles:
             taps = [proto[tap, :, r * tile : (r + 1) * tile].reshape(16, SIDE).astype(FT) for tap in range(4)]
             seen = []
-            for k in range(-3, count):
+            for k in range(first - 3, last):
                 start = pl.multiple_of((base + k + 3) * frame + r * tile, tile)
                 seen.append(xbuf[:, pl.ds(start, tile)].reshape(16, SIDE).astype(FT))
-                if k >= 0:
-                    acc = (seen[k] * taps[0] + seen[k + 1] * taps[1]) + (seen[k + 2] * taps[2] + seen[k + 3] * taps[3])
+                if k >= first:
+                    acc = (seen[-4] * taps[0] + seen[-3] * taps[1]) + (seen[-2] * taps[2] + seen[-1] * taps[3])
                     ybuf[k // 2, r * 16 : (r + 1) * 16, k % 2 * SIDE : (k % 2 + 1) * SIDE] = acc.astype(BF16)
 
     def dots(ybuf, base, s, count, keep=None):
@@ -185,11 +195,13 @@
     pl.semaphore_wait(barrier, len(senders))
     if slabs > 1:
         history_copy().start()
-    raw_copy(0).wait()
+    opening(0).wait()
     for copy in taps:
         copy.wait()
     raw_copy(AHEAD).start()
-    fir(yone, 0, range(8))
+    fir(yone, 0, range(8), 0, CHUNK // 2)
+    opening(1).wait()
+    fir(yone, 0, range(8), CHUNK // 2, CHUNK)
     for copy in constants[:4]:
         copy.wait()
 
@@ -219,14 +231,15 @@
     if slabs > 1:
         history_copy().wait()
         xbuf[:, : 3 * frame] = jnp.where(tm > 0, history[...], 0.0)
-    fir(yone, 0, range(8), FIRST)
+    fir(yone, 0, range(8), 0, FIRST)
     for s in range(0, CHUNK, 2 * GROUP):
         dots(ytwo, base + CHUNK, s, GROUP)
     dots(yone, 0, 0, FIRST // 2)
 
+    band_out[...] = jnp.concatenate([band_ref[...], jnp.zeros((FS - FR, SIDE), F32)], 0).astype(BF16)
     copies = []
     for off in range(1, slabs):
-        copy = remote(band_ref, bands.at[off - 1], band_send.at[off - 1], band_recv.at[off - 1], peer(off, 0))
+        copy = remote(band_out, bands.at[off - 1], band_send.at[off - 1], band_recv.at[off - 1], peer(off, 0))
         copy.start()
         copies.append(copy)
 
@@ -238,16 +251,14 @@
     spread = jnp.concatenate([lane == spot, lane == NBLK - 1 - spot], 1).astype(F32).astype(BF16)
     late = jnp.dot(delays_ref[...].astype(F32).astype(BF16), spread, preferred_element_type=F32)
     line = iota((quad, 2 * SIDE), 0) // trials
-    masks = [
-        jnp.concatenate(
+    for g in range(groups):
+        masks[g] = jnp.concatenate(
             [
                 jnp.where((late == float(v)) & (line == g), 1.0, 0.0)
                 for v in range(MAXT + 1)
             ],
             0,
         ).astype(BF16)
-        for g in range(groups)
-    ]
 
     def column(ref):
         n = ref.shape[1]
@@ -261,18 +272,18 @@
     rank = jnp.sum(jnp.where((owner == mine) & (row < lane // trials), 1, 0), 0, keepdims=True)
     place = (mine * slots + rank) * trials + lane[:1] % trials
     pack = jnp.where(iota((owner_count * rows, lanes), 0) == place, 1.0, 0.0)
-    pack = jnp.concatenate([pack, pack], 1).astype(BF16)
+    pack_ref[...] = jnp.concatenate([pack, pack], 1).astype(BF16)
 
     reach = jnp.broadcast_to(column(widths_ref), (boxes, SIDE))
     root = 1.0 / jnp.sqrt(reach.astype(F32))
-    root = jnp.concatenate([root] * rows, 0)
+    root_ref[...] = jnp.concatenate([root] * rows, 0)
     reach = jnp.concatenate([reach] * rows, 0)
     if WMAX * rows > SIDE:
         reach = jnp.broadcast_to(reach[:, :1], (boxes * rows, WMAX * rows))
     lag = iota((boxes * rows, WMAX * rows), 1)
     series = iota((boxes * rows, WMAX * rows), 0) // boxes
     kernel = jnp.where((lag % rows == series) & (lag // rows < reach), 1.0, 0.0)
-    kernel = jnp.concatenate([kernel, kernel], 1).astype(BF16)
+    kernel_ref[...] = kernel.astype(BF16)
     used = (spec + FD - 1) * groups
     direct[used:] = jnp.zeros((direct.shape[0] - used, SIDE), F32)
     mirror[used:] = jnp.zeros((direct.shape[0] - used, SIDE), F32)
@@ -280,7 +291,7 @@
     band = band_ref[...]
     for off in range(1, slabs):
         copies[off - 1].wait()
-        band = band + bands[off - 1]
+        band = band + bands[off - 1].astype(F32)[:FR]
     scale = 1.0 / (4 * frame)
     held = iota((FR, SIDE), 0) <= HALF
     inv[...] = jnp.where(held, scale / (band * (scale / spectra) + 1e-06), 0.0)
@@ -345,7 +356,7 @@
         high = dd.astype(BF16)
         low = (dd - high.astype(F32)).astype(BF16)
         return lax.dot_general(
-            pack, jnp.concatenate([high, low], 1), (((1,), (1,)), ((), ())), preferred_element_type=F32
+            pack_ref[...], jnp.concatenate([high, low], 1), (((1,), (1,)), ((), ())), preferred_element_type=F32
         )
 
     blocks = spec // SPB
@@ -356,10 +367,12 @@
         direct[(spec + d) * groups : (spec + d + 1) * groups] = carry[d]
         mirror[(spec + d) * groups : (spec + d + 1) * groups] = carry[FD - 1 + d]
     copies = []
+    half = middle * SPB
+    upper = series(half, count - half)
     if slabs > 1:
         reach = (MAXT + 1) * TT
-        late = series(spec - reach, count - spec + reach)
-        sendb[...] = gather(late, reach - TT, count - spec + reach).reshape(sendb.shape)
+        late = upper[spec - reach - half :]
+        sendb[...] = gather(late, reach - TT, count - spec + reach).reshape(sendb.shape).astype(BF16)
         for off in range(owner_count - 1, -1, -1):
             copy = remote(
                 sendb.at[lax.rem(dm + off, owner_count)], gotb.at[dm],
@@ -372,7 +385,9 @@
         start = (middle * SPB + d) * groups
         direct[start : start + groups] += carry[d]
         mirror[start : start + groups] += carry[FD - 1 + d]
-    send[...] = gather(series(0, spec), 0, spec).reshape(send.shape)
+    lower = series(0, half + 16)
+    each = jnp.concatenate([lower, upper[16 : spec - half]], 0)
+    send[...] = gather(each, 0, spec).reshape(send.shape).astype(BF16)
     for off in range(1, owner_count):
         copy = remote(
             send.at[lax.rem(dm + off, owner_count)], got.at[dm],
@@ -387,9 +402,9 @@
     lane = iota((rows, SIDE), 1)
     stacks = []
     for d in range(owner_count):
-        own = got[d]
+        own = got[d].astype(F32)
         if slabs > 1:
-            past = pltpu.roll(jnp.where(tm > 0, gotb[d], 0.0), SIDE - TT, 1)
+            past = pltpu.roll(jnp.where(tm > 0, gotb[d].astype(F32), 0.0), SIDE - TT, 1)
             own = own + jnp.where(lane < SIDE - TT, past, 0.0)
         else:
             past = jnp.zeros((rows, SIDE), F32)
@@ -397,12 +412,10 @@
         for lag in range(1, WMAX):
             moved.append(pltpu.roll(jnp.where(lane < SIDE - lag, own, past), lag, 1))
         stacks.append(jnp.concatenate(moved, 0))
-    stack = jnp.concatenate(stacks, 1)
-    high = stack.astype(BF16)
-    low = (stack - high.astype(F32)).astype(BF16)
-    box = jnp.dot(kernel, jnp.concatenate([high, low], 0), preferred_element_type=F32)
+    stack = jnp.concatenate(stacks, 1).astype(BF16)
+    box = jnp.dot(kernel_ref[...], stack, preferred_element_type=F32)
     for d in range(owner_count):
-        done = (box[:, d * SIDE : (d + 1) * SIDE] * root).astype(BF16)
+        done = (box[:, d * SIDE : (d + 1) * SIDE] * root_ref[...]).astype(BF16)
         for s in range(slots):
             out_ref[s, d] = done[s * trials * boxes : (s + 1) * trials * boxes]
 
@@ -417,7 +430,9 @@
     masks = fine_rows(groups, channels // NBLK)
     sizes = (spec * slabs, spec, groups, slabs, owner_count, axes)
     rows = -(-(spec + FD - 1) // 8) * 8
-    block = pltpu.VMEM((owner_count, capacity * trials, SIDE), F32)
+    lanes = (MAXT + 1) * groups * trials
+    boxes = widths.shape[0]
+    block = pltpu.VMEM((owner_count, capacity * trials, SIDE), BF16)
     sems = lambda n: pltpu.SemaphoreType.DMA((max(n, 1),))
     small = [w1, w2, tw, last, masks, delays.reshape(groups * trials, NBLK), widths[None], owners.T]
     out = (capacity, owner_count, trials * widths.shape[0], spec)
@@ -435,7 +450,8 @@
             pltpu.VMEM((1, 3 * channels), BF16),
             pltpu.VMEM((spec * FR, SIDE), F32),
             pltpu.VMEM((FR, SIDE), F32),
-            pltpu.VMEM((max(slabs - 1, 1), FR, SIDE), F32),
+            pltpu.VMEM((FS, SIDE), BF16),
+            pltpu.VMEM((max(slabs - 1, 1), FS, SIDE), BF16),
             pltpu.VMEM((FR, SIDE), F32),
             pltpu.VMEM((rows * groups, SIDE), F32),
             pltpu.VMEM((rows * groups, SIDE), F32),
@@ -443,6 +459,11 @@
             block,
             block,
             block,
+            pltpu.VMEM((groups, lanes, 2 * SIDE), BF16),
+            pltpu.VMEM((owner_count * capacity * trials, 2 * lanes), BF16),
+            pltpu.VMEM((boxes * capacity * trials, WMAX * capacity * trials), BF16),
+            pltpu.VMEM((boxes * capacity * trials, SIDE), F32),
+            sems(2),
             sems(spec // CHUNK),
             sems(taps),
             sems(len(small)),

time: 22.2 us -> 21.8 us (0.982)
  Pallas kernels: 21.4 us -> 21 us
    pallas_call x1, Pallas kernels: 21.4 us -> 21 us  [shards(): pl.pallas_call(functools.partial(search_kernel, sizes), in_specs=[pl.Bloc...]
where the time goes in v6:
time: 21.8 us; the launch traced here: 21.7 us
  Pallas kernels  21 us (96%)
  local copies, waits for them, and re-layouts  0.66 us (3%)
    pallas_call x1, Pallas kernels, shards(): pl.pallas_call(functools.partial(search_kernel, sizes), in_specs=[pl.Bloc...  21 us
    unnamed x1, local copies, waits for them, and re-layouts  0.66 us

profile of v6, /device:TPU:0, one launch (start us, length us, event | category | flops | bytes accessed | tf_op | source)
XLA Modules:
  0.0 21.7 jit_solution(10386483186711497566)
XLA Ops:
  0.0 21.0 %search.1 = bf16[4,4,32,128]{3,2,1,0:T(8,128)(2,1)S(1)} custom-call(bf16[1,2097152]{1,0:T(2,128)(2,1)} %raw_ref.1, f32[4,16384]{1,0:T(4,128)} %proto_ref.1, bf16[144,128]{1,0:T(8,128)(2,1)} %constant.10.clone.w1_any, bf16[256,256]{1,0:T(8,128)(2,1)} %constant.11.clone.w2_any, bf16[2,64,128]{2,1,0:T(8,128)(2,1)} %constant.12.clone.tw_any, ...), custom_call_target="tpu_custom_call" | custom-call | tf_op jit(solution)/shard_map/search/pallas_call | solution.py:439
  21.0 0.7 %copy.13 = bf16[4,4,1,4,8,128]{5,4,3,2,1,0:T(8,128)(2,1)} copy(bf16[4,4,1,4,8,128]{5,4,3,2,1,0:T(8,128)(2,1)S(1)} %bitcast.6) | data formatting | bytes 262144

commit v7 on v6

--- a/solution.py
+++ b/solution.py
@@ -60,7 +60,7 @@
 def search_kernel(
     sizes, raw_ref, proto_ref, w1_any, w2_any, tw_any, last_any, m_any, delays_any, widths_any, owners_any, out_ref,
     xbuf, proto, w1_ref, w2_ref, tw_ref, last_ref, m_ref, delays_ref, widths_ref, owners_ref,
-    yone, ytwo, history, p_ref, band_ref, band_out, bands, inv, direct, mirror, send, sendb, got, gotb,
+    yone, ytwo, hist_raw, hist_out, history, p_ref, band_ref, band_out, bands, inv, direct, mirror, send, sendb, got, gotb,
     masks, pack_ref, kernel_ref, root_ref, open_sem, raw_sem, proto_sem, const_sem,
     hist_send, hist_recv, band_send, band_recv, own_send, own_recv, next_send, next_recv,
 ):
@@ -102,10 +102,13 @@
         )
 
     def history_copy():
-        size = history.shape[1]
-        last = raw_ref.at[:, pl.ds(spec * frame - size, size)]
-        return remote(last, history, hist_send, hist_recv, peer(1, 0))
-
+        return remote(hist_out, history, hist_send, hist_recv, peer(1, 0))
+
+    ending = pltpu.make_async_copy(
+        raw_ref.at[:, pl.ds((spec - 3) * frame, 3 * frame)], hist_raw, open_sem.at[2]
+    )
+    if slabs > 1:
+        ending.start()
     taps = [
         pltpu.make_async_copy(proto_ref.at[tap : tap + 1], proto.at[tap], proto_sem.at[tap])
         for tap in range(4)
@@ -144,11 +147,15 @@
 
     tile = 16 * SIDE
 
-    def fir(ybuf, base, tiles, first=0, last=CHUNK):
+    def fir(ybuf, base, tiles, first=0, last=CHUNK, past=False):
         for r in tiles:
             taps = [proto[tap, :, r * tile : (r + 1) * tile].reshape(16, SIDE).astype(FT) for tap in range(4)]
             seen = []
             for k in range(first - 3, last):
+                if past and k < 0:
+                    row = (k + 3) * SIDE + r * 16
+                    seen.append(jnp.where(tm > 0, history[row : row + 16].astype(F32), 0.0).astype(FT))
+                    continue
                 start = pl.multiple_of((base + k + 3) * frame + r * tile, tile)
                 seen.append(xbuf[:, pl.ds(start, tile)].reshape(16, SIDE).astype(FT))
                 if k >= first:
@@ -192,6 +199,9 @@
             dots(ybuf, base, 2 * GROUP * u, GROUP, keep if u == 0 else None)
             fir(ynext, following, range(8 * u // units, 8 * (u + 1) // units))
 
+    if slabs > 1:
+        ending.wait()
+        hist_out[...] = hist_raw[...].reshape(3 * SIDE, SIDE)
     pl.semaphore_wait(barrier, len(senders))
     if slabs > 1:
         history_copy().start()
@@ -230,8 +240,7 @@
     stage(yone, base, ytwo, base + CHUNK)
     if slabs > 1:
         history_copy().wait()
-        xbuf[:, : 3 * frame] = jnp.where(tm > 0, history[...], 0.0)
-    fir(yone, 0, range(8), 0, FIRST)
+    fir(yone, 0, range(8), 0, FIRST, slabs > 1)
     for s in range(0, CHUNK, 2 * GROUP):
         dots(ytwo, base + CHUNK, s, GROUP)
     dots(yone, 0, 0, FIRST // 2)
@@ -448,6 +457,8 @@
             pltpu.VMEM((CHUNK // 2, SIDE, 2 * SIDE), BF16),
             pltpu.VMEM((CHUNK // 2, SIDE, 2 * SIDE), BF16),
             pltpu.VMEM((1, 3 * channels), BF16),
+            pltpu.VMEM((3 * SIDE, SIDE), BF16),
+            pltpu.VMEM((3 * SIDE, SIDE), BF16),
             pltpu.VMEM((spec * FR, SIDE), F32),
             pltpu.VMEM((FR, SIDE), F32),
             pltpu.VMEM((FS, SIDE), BF16),
@@ -463,7 +474,7 @@
             pltpu.VMEM((owner_count * capacity * trials, 2 * lanes), BF16),
             pltpu.VMEM((boxes * capacity * trials, WMAX * capacity * trials), BF16),
             pltpu.VMEM((boxes * capacity * trials, SIDE), F32),
-            sems(2),
+            sems(3),
             sems(spec // CHUNK),
             sems(taps),
             sems(len(small)),

time: 21.8 us -> 21.3 us (0.977)
  Pallas kernels: 21 us -> 20.5 us
    pallas_call x1, Pallas kernels: 21 us -> 20.5 us  [shards(): pl.pallas_call(functools.partial(search_kernel, sizes), in_specs=[pl.Bloc...]
where the time goes in v7:
time: 21.3 us; the launch traced here: 21.2 us
  Pallas kernels  20.5 us (96%)
  local copies, waits for them, and re-layouts  0.66 us (3%)
    pallas_call x1, Pallas kernels, shards(): pl.pallas_call(functools.partial(search_kernel, sizes), in_specs=[pl.Bloc...  20.5 us
    unnamed x1, local copies, waits for them, and re-layouts  0.66 us

profile of v7, /device:TPU:0, one launch (start us, length us, event | category | flops | bytes accessed | tf_op | source)
XLA Modules:
  0.0 21.2 jit_solution(16804447545549387522)
XLA Ops:
  0.0 20.5 %search.1 = bf16[4,4,32,128]{3,2,1,0:T(8,128)(2,1)S(1)} custom-call(bf16[1,2097152]{1,0:T(2,128)(2,1)} %raw_ref.1, f32[4,16384]{1,0:T(4,128)} %proto_ref.1, bf16[144,128]{1,0:T(8,128)(2,1)} %constant.10.clone.w1_any, bf16[256,256]{1,0:T(8,128)(2,1)} %constant.11.clone.w2_any, bf16[2,64,128]{2,1,0:T(8,128)(2,1)} %constant.12.clone.tw_any, ...), custom_call_target="tpu_custom_call" | custom-call | tf_op jit(solution)/shard_map/search/pallas_call | solution.py:448
  20.5 0.7 %copy.13 = bf16[4,4,1,4,8,128]{5,4,3,2,1,0:T(8,128)(2,1)} copy(bf16[4,4,1,4,8,128]{5,4,3,2,1,0:T(8,128)(2,1)S(1)} %bitcast.6) | data formatting | bytes 262144

commit v8 on v7

--- a/solution.py
+++ b/solution.py
@@ -202,14 +202,14 @@
     if slabs > 1:
         ending.wait()
         hist_out[...] = hist_raw[...].reshape(3 * SIDE, SIDE)
-    pl.semaphore_wait(barrier, len(senders))
-    if slabs > 1:
-        history_copy().start()
     opening(0).wait()
     for copy in taps:
         copy.wait()
     raw_copy(AHEAD).start()
     fir(yone, 0, range(8), 0, CHUNK // 2)
+    pl.semaphore_wait(barrier, len(senders))
+    if slabs > 1:
+        history_copy().start()
     opening(1).wait()
     fir(yone, 0, range(8), CHUNK // 2, CHUNK)
     for copy in constants[:4]:

time: 21.3 us -> 21.3 us (level)
  no operation moved by 1% of the time
where the time goes in v8:
time: 21.3 us; the launch traced here: 21.2 us
  Pallas kernels  20.5 us (96%)
  local copies, waits for them, and re-layouts  0.66 us (3%)
    pallas_call x1, Pallas kernels, shards(): pl.pallas_call(functools.partial(search_kernel, sizes), in_specs=[pl.Bloc...  20.5 us
    unnamed x1, local copies, waits for them, and re-layouts  0.66 us

profile of v8, /device:TPU:0, one launch (start us, length us, event | category | flops | bytes accessed | tf_op | source)
XLA Modules:
  0.0 21.2 jit_solution(13783449477075517364)
XLA Ops:
  0.0 20.5 %search.1 = bf16[4,4,32,128]{3,2,1,0:T(8,128)(2,1)S(1)} custom-call(bf16[1,2097152]{1,0:T(2,128)(2,1)} %raw_ref.1, f32[4,16384]{1,0:T(4,128)} %proto_ref.1, bf16[144,128]{1,0:T(8,128)(2,1)} %constant.10.clone.w1_any, bf16[256,256]{1,0:T(8,128)(2,1)} %constant.11.clone.w2_any, bf16[2,64,128]{2,1,0:T(8,128)(2,1)} %constant.12.clone.tw_any, ...), custom_call_target="tpu_custom_call" | custom-call | tf_op jit(solution)/shard_map/search/pallas_call | solution.py:448
  20.5 0.7 %copy.13 = bf16[4,4,1,4,8,128]{5,4,3,2,1,0:T(8,128)(2,1)} copy(bf16[4,4,1,4,8,128]{5,4,3,2,1,0:T(8,128)(2,1)S(1)} %bitcast.6) | data formatting | bytes 262144
